TPU v7x, 32 devices: a whole 2x2x4 slice. The times are simulated.
32 devices in a mesh: lat: 8 (over z, x), lon: 4 (over y, core).
Axes of the slice: x: 2, y: 2, z: 4, core: 2. Of those that a mesh axis runs over, the one named last changes fastest.
Arguments:
- zonal_wind: float32 [64, 72, 2880], P('lat', None, 'lon'), may hold values from -6 to 6
- merid_wind: float32 [64, 72, 2880], P('lat', None, 'lon'), may hold values from -6 to 6
- pressure: float32 [64, 72, 2880], P('lat', None, 'lon'), may hold values from -6 to 6
- zonal_metric: float32 [64], P('lat'), may hold values from 0.2 to 1
- helm_inverse: float32 [64, 72, 72], P('lat'), may hold values from -0.06 to 1.06
- kernel_taps: float32 [16, 512], replicated, may hold values from 0.05 to 1
- filter_width: int32 [16], replicated, may hold values from 16 to 256
Outputs:
- zonal_out: float32 [64, 72, 2880], P('lat', None, 'lon')
- merid_out: float32 [64, 72, 2880], P('lat', None, 'lon')
- pressure_out: float32 [64, 72, 2880], P('lat', None, 'lon')
All inputs are finite; a program needn't handle non-finite values.
Results may differ from a plain program's by a relative error of at most 0.0001.
Values sent between devices are 32-bit elements; how exact they have to be, the bound alone decides.
A program may use at most 128 MiB of HBM per device.

v0:
```python
import jax
import jax.numpy as jnp
from jax import lax
from jax.sharding import PartitionSpec as P

meridional = 0.5
compress = 0.5


def from_partner(block, axis, distance):
    count = lax.axis_size(axis)
    route = []
    for low in range(count):
        high = low | 1 << distance
        if high != low and high < count:
            route += [(low, high), (high, low)]
    return lax.ppermute(block, axis, route)


def extended(value, sides, width, wrap):
    for axis, dim in sides:
        peers, length = (lax.axis_size(axis), value.shape[dim])
        up = [(i, (i + 1) % peers) for i in range(peers if wrap else peers - 1)]
        down = [(j, i) for i, j in up]
        last = lax.slice_in_dim(value, length - width, length, axis=dim)
        initial = lax.slice_in_dim(value, 0, width, axis=dim)
        before = lax.ppermute(last, axis, up)
        after = lax.ppermute(initial, axis, down)
        value = jnp.concatenate([before, value, after], axis=dim)
    return value


def kernels(kernel_taps, filter_width):
    tap_count = kernel_taps.shape[1]
    offsets = jnp.abs(jnp.arange(tap_count, dtype=jnp.int32) - tap_count // 2)
    kept_taps = jnp.where(
        offsets[None, :] <= filter_width[:, None], kernel_taps, jnp.zeros_like(kernel_taps)
    )
    return kept_taps / jnp.sum(kept_taps, axis=1, keepdims=True)


def toeplitz(weight_row, outputs):
    tap_count = weight_row.shape[0]
    padded = jnp.concatenate([weight_row, jnp.zeros((outputs + 1,), weight_row.dtype)])
    tiled = jnp.tile(padded, outputs)[: outputs * (outputs + tap_count)]
    return tiled.reshape(outputs, outputs + tap_count)


def filter_rows(windows, weights):
    outputs = windows.shape[-1] - weights.shape[-1]

    def one_row(packed):
        window_row, weight_row = packed
        matrix = toeplitz(weight_row, outputs)
        return jnp.einsum("vbk,ok->vbo", window_row, matrix, precision=lax.Precision.HIGHEST)

    return lax.map(one_row, (windows, weights))


def row_windows(values, outputs, half_span):
    padded = jnp.concatenate([values[..., -half_span:], values, values[..., :half_span]], axis=-1)
    segments = values.shape[-1] // outputs
    pieces = [
        padded[..., segment * outputs : segment * outputs + outputs + 2 * half_span]
        for segment in range(segments)
    ]
    return jnp.stack(pieces, axis=-2)


def lat_neighbours(values, sign_flip):
    edges = jnp.stack([values[0], values[-1]])
    partner = from_partner(edges, "lon", lax.axis_size("lon").bit_length() - 2)
    padded = extended(values, (("lat", 0),), 1, False)
    lat_index = lax.axis_index("lat")
    lat_count = lax.axis_size("lat")
    lower_rim = jnp.where(lat_index == 0, sign_flip * partner[0], padded[0])
    upper_rim = jnp.where(lat_index == lat_count - 1, sign_flip * partner[1], padded[-1])
    south_rows = jnp.concatenate([lower_rim[None], padded[1:-2]], axis=0)
    north_rows = jnp.concatenate([padded[2:-1], upper_rim[None]], axis=0)
    return (south_rows, north_rows)


def lon_difference(values):
    padded = extended(values, (("lon", 2),), 1, True)
    return 0.5 * (padded[..., 2:] - padded[..., :-2])


def polar_filter(tendency, weights):
    row_count, vector_count, col_count = tendency.shape
    half_span = weights.shape[1] // 2
    lon_index = lax.axis_index("lon")
    lon_count = lax.axis_size("lon")
    row_share = row_count // lon_count
    sectioned = tendency.reshape(1, row_count, vector_count, col_count)
    spread = lax.all_to_all(
        lax.all_to_all(sectioned, "lat", split_axis=2, concat_axis=0, tiled=True),
        "lon",
        split_axis=1,
        concat_axis=3,
        tiled=True,
    )
    first_row = lon_index * row_share
    south_weights = lax.dynamic_slice_in_dim(weights, first_row, row_share, 0)
    north_weights = lax.dynamic_slice_in_dim(weights, row_count + first_row, row_share, 0)
    picked = jnp.concatenate([spread[0], spread[-1]], axis=0)
    chosen = jnp.concatenate([south_weights, north_weights], axis=0)
    filtered = filter_rows(row_windows(picked, col_count, half_span), chosen).reshape(picked.shape)
    spread = spread.at[0].set(filtered[:row_share]).at[-1].set(filtered[row_share:])
    returned = lax.all_to_all(
        lax.all_to_all(spread, "lat", split_axis=0, concat_axis=2, tiled=True),
        "lon",
        split_axis=3,
        concat_axis=1,
        tiled=True,
    )
    return returned.reshape(row_count, vector_count, col_count)


def on_device(
    zonal_wind, merid_wind, pressure, zonal_metric, helm_inverse, kernel_taps, filter_width
):
    weights = kernels(kernel_taps, filter_width)
    metric = zonal_metric[:, None, None]
    level_count = pressure.shape[1]
    zonal_next = zonal_wind
    merid_next = merid_wind
    pressure_next = pressure
    for step_index in range(2):
        south_rows, north_rows = lat_neighbours(pressure_next, 1.0)
        tend_u = -metric * lon_difference(pressure_next)
        tend_v = -meridional * 0.5 * (north_rows - south_rows)
        smoothed = polar_filter(jnp.concatenate([tend_u, tend_v], axis=1), weights)
        zonal_next = zonal_next + smoothed[:, :level_count]
        merid_next = merid_next + smoothed[:, level_count:]
        south_rows, north_rows = lat_neighbours(merid_next, -1.0)
        divergence = metric * lon_difference(zonal_next) + meridional * 0.5 * (
            north_rows - south_rows
        )
        source = pressure_next - compress * divergence
        pressure_next = jnp.einsum(
            "rkl,rlc->rkc", helm_inverse, source, precision=lax.Precision.HIGHEST
        )
    return (zonal_next, merid_next, pressure_next)


def solution(mesh):
    return jax.shard_map(
        on_device,
        mesh=mesh,
        in_specs=(
            P("lat", None, "lon"),
            P("lat", None, "lon"),
            P("lat", None, "lon"),
            P("lat"),
            P("lat", None, None),
            P(),
            P(),
        ),
        out_specs=(P("lat", None, "lon"), P("lat", None, "lon"), P("lat", None, "lon")),
        check_vma=False,
    )
```

profile of v0, /device:TPU:0, one launch (start us, length us, event | category | flops | bytes accessed | tf_op | source)
XLA Modules:
  0.0 989.3 jit_solution(8293058266000766947)
XLA Ops:
  14.8 10.6 %collective-permute-done.1 = f32[8,72,1]{2,1,0:T(8,128)} collective-permute-done((f32[8,72,1]{2,1,0:T(8,128)}, f32[8,72,1]{2,1,0:T(8,128)}, u32[]{:S(2)}, u32[]{:S(2)}) %collective-permute-start.1) | collective-permute-done | bytes 2336 | tf_op jit(solution)/shard_map/ppermute | solution.py:27
  32.0 86.8 %all_to_all.138 = f32[1,8,144,720]{3,1,0,2:T(8,128)S(1)} all-to-all(f32[1,8,144,720]{3,1,0,2:T(8,128)S(1)} %copy.68), channel_id=1, replica_groups=mesh['lat'=8,'lon'=4] {'lat'}, dimensions={2} | all-to-all | bytes 6635520 | tf_op jit(solution)/shard_map/all_to_all | solution.py:96
  128.1 40.9 %all-to-all-done.1 = f32[8,8,18,720]{3,0,2,1:T(8,128)} async-done(((f32[8,8,18,720]{3,0,2,1:T(8,128)}), f32[8,8,18,720]{3,0,2,1:T(8,128)}, u32[]{:S(2)}, u32[]{:S(2)}) %all-to-all-start.1) | async-done | bytes 3317792 | tf_op jit(solution)/shard_map/all_to_all | solution.py:95
  190.7 79.7 %while.24 = (s32[]{:T(128)}, f32[4,18,4,720]{3,1,2,0:T(8,128)S(1)}, f32[4,18,4,1232]{3,0,1,2:T(4,128)S(1)}, f32[4,512]{1,0:T(4,128)S(1)}, s32[]{:T(128)}, /*index=5*/f32[]{:T(128)}) while((s32[]{:T(128)}, f32[4,18,4,720]{3,1,2,0:T(8,128)S(1)}, f32[4,18,4,1232]{3,0,1,2:T(4,128)S(1)}, f32[4,512]{1,0:T(4,128)S(1)}, s32[]{:T(128)}, ...), condition=%wide.region_2.3_spmd, body=%wide.region_1.2_spmd.sunk | while | flops 766402560 | bytes 22686884 | solution.py:57
  193.3 6.2 tile.23
  213.1 6.2 tile.23
  232.9 6.2 tile.23
  252.7 6.2 tile.23
  272.5 8.5 scatter.14
  281.0 8.5 scatter.15
  293.2 79.6 %all_to_all.139 = f32[8,2,18,2880]{3,1,2,0:T(2,128)} all-to-all(f32[8,2,18,2880]{3,1,2,0:T(2,128)S(1)} %copy.77), channel_id=1, replica_groups=mesh['lat'=8,'lon'=4] {'lat'}, dimensions={0} | all-to-all | bytes 6635520 | tf_op jit(solution)/shard_map/all_to_all | solution.py:110
  372.9 11.7 %copy.78 = f32[1,2,144,2880]{2,1,0,3:T(2,128)} copy(f32[1,2,144,2880]{3,1,2,0:T(2,128)} %bitcast.130) | data formatting | bytes 6635520 | tf_op jit(solution)/shard_map/all_to_all | solution.py:110
  384.5 73.0 %all_to_all.140 = f32[1,2,144,2880]{2,1,0,3:T(2,128)} all-to-all(f32[1,2,144,2880]{2,1,0,3:T(2,128)} %copy.78), channel_id=1, replica_groups=mesh['lat'=8,'lon'=4] {'lon'}, dimensions={3} | all-to-all | bytes 6635520 | tf_op jit(solution)/shard_map/all_to_all | solution.py:109
  457.5 9.7 copy.97
  503.0 16.2 %collective-permute-done.11 = f32[8,72,1]{2,1,0:T(8,128)S(1)} collective-permute-done((f32[8,72,1]{2,1,0:T(8,128)S(1)}, f32[8,72,1]{2,1,0:T(8,128)S(1)}, u32[]{:S(2)}, u32[]{:S(2)}) %collective-permute-start.11) | collective-permute-done | bytes 2336 | tf_op jit(solution)/shard_map/ppermute | solution.py:27
  523.1 85.1 %all_to_all.141 = f32[1,8,144,720]{3,1,0,2:T(8,128)S(1)} all-to-all(f32[1,8,144,720]{3,1,0,2:T(8,128)S(1)} %copy.81), channel_id=1, replica_groups=mesh['lat'=8,'lon'=4] {'lat'}, dimensions={2} | all-to-all | bytes 6635520 | tf_op jit(solution)/shard_map/all_to_all | solution.py:96
  616.8 41.2 %all-to-all-done.5 = f32[8,8,18,720]{3,0,2,1:T(8,128)} async-done(((f32[8,8,18,720]{3,0,2,1:T(8,128)}), f32[8,8,18,720]{3,0,2,1:T(8,128)}, u32[]{:S(2)}, u32[]{:S(2)}) %all-to-all-start.5) | async-done | bytes 3317792 | tf_op jit(solution)/shard_map/all_to_all | solution.py:95
  680.8 82.3 %while.25 = (s32[]{:T(128)}, f32[4,18,4,720]{3,1,2,0:T(8,128)}, f32[4,18,4,1232]{3,0,1,2:T(4,128)S(1)}, f32[4,512]{1,0:T(4,128)S(1)}, s32[]{:T(128)}, /*index=5*/f32[]{:T(128)}) while((s32[]{:T(128)}, f32[4,18,4,720]{3,1,2,0:T(8,128)}, f32[4,18,4,1232]{3,0,1,2:T(4,128)S(1)}, f32[4,512]{1,0:T(4,128)S(1)}, s32[]{:T(128)}, ...), condition=%wide.region_4.5_spmd, body=%wide.region_3.4_spmd.sunk | while | flops 766402560 | bytes 22811300 | solution.py:57
  683.3 6.2 tile.25
  695.5 6.2 fusion.107
  703.8 6.2 tile.25
  716.0 6.2 fusion.107
  724.3 6.2 tile.25
  736.5 6.2 fusion.107
  744.7 6.2 tile.25
  757.0 6.2 fusion.107
  766.5 8.5 scatter.16
  775.0 8.6 scatter.19
  787.3 79.3 %all_to_all.142 = f32[8,2,18,2880]{3,1,2,0:T(2,128)} all-to-all(f32[8,2,18,2880]{3,1,2,0:T(2,128)S(1)} %copy.90), channel_id=1, replica_groups=mesh['lat'=8,'lon'=4] {'lat'}, dimensions={0} | all-to-all | bytes 6635520 | tf_op jit(solution)/shard_map/all_to_all | solution.py:110
  866.6 11.7 %copy.91 = f32[1,2,144,2880]{2,1,0,3:T(2,128)} copy(f32[1,2,144,2880]{3,1,2,0:T(2,128)} %bitcast.131) | data formatting | bytes 6635520 | tf_op jit(solution)/shard_map/all_to_all | solution.py:110
  878.3 73.0 %all_to_all.143 = f32[1,2,144,2880]{2,1,0,3:T(2,128)} all-to-all(f32[1,2,144,2880]{2,1,0,3:T(2,128)} %copy.91), channel_id=1, replica_groups=mesh['lat'=8,'lon'=4] {'lon'}, dimensions={3} | all-to-all | bytes 6635520 | tf_op jit(solution)/shard_map/all_to_all | solution.py:109
  951.3 9.7 copy.101
  (188 shorter events, 250.2 us)
Async XLA Ops:
  0.6 490.7 %copy-start = (f32[8,72,72]{2,1,0:T(8,128)S(1)}, f32[8,72,72]{2,1,0:T(8,128)}, u32[]{:S(2)}) copy-start(f32[8,72,72]{2,1,0:T(8,128)} %param.23) | copy-start | bytes 497668
  0.6 9.7 copy-start.1
  1.9 26.3 %collective-permute-start.4 = (f32[1,72,720]{2,1,0:T(8,128)S(1)}, f32[1,72,720]{2,1,0:T(8,128)}, u32[]{:S(2)}, u32[]{:S(2)}) collective-permute-start(f32[1,72,720]{2,1,0:T(8,128)S(1)} %get-tuple-element.167), channel_id=1, source_target_pairs={{0,4},{4,8},{8,12},{12,16},{16,20},{20,24},{24,28},{1,5},{5,9},{9,... | collective-permute-start | bytes 622088 | tf_op jit(solution)/shard_map/ppermute | solution.py:27
  7.4 20.8 %collective-permute-start.3 = (f32[1,72,720]{2,1,0:T(8,128)S(1)}, f32[1,72,720]{2,1,0:T(8,128)}, u32[]{:S(2)}, u32[]{:S(2)}) collective-permute-start(f32[1,72,720]{2,1,0:T(8,128)S(1)} %get-tuple-element.168), channel_id=1, source_target_pairs={{4,0},{8,4},{12,8},{16,12},{20,16},{24,20},{28,24},{5,1},{9,5},{13... | collective-permute-start | bytes 622088 | tf_op jit(solution)/shard_map/ppermute | solution.py:28
  8.8 19.4 %collective-permute-start.2 = (f32[2,72,720]{2,1,0:T(8,128)S(1)}, f32[2,72,720]{2,1,0:T(8,128)S(1)}, u32[]{:S(2)}, u32[]{:S(2)}) collective-permute-start(f32[2,72,720]{2,1,0:T(8,128)S(1)} %pad_maximum_fusion.12), channel_id=1, source_target_pairs={{0,2},{2,0},{1,3},{3,1},{4,6},{6,4},{5,7},{7,5},{8,10},{10,8},{9,1... | collective-permute-start | bytes 1244168 | tf_op jit(solution)/shard_map/ppermute | solution.py:17
  11.2 14.2 %collective-permute-start.1 = (f32[8,72,1]{2,1,0:T(8,128)}, f32[8,72,1]{2,1,0:T(8,128)}, u32[]{:S(2)}, u32[]{:S(2)}) collective-permute-start(f32[8,72,1]{2,1,0:T(8,128)} %get-tuple-element.164), channel_id=1, source_target_pairs={{0,1},{1,2},{2,3},{3,0},{4,5},{5,6},{6,7},{7,4},{8,9},{9,10},{10,1... | collective-permute-start | bytes 6920 | tf_op jit(solution)/shard_map/ppermute | solution.py:27
  11.2 3.6 copy-start.15
  11.2 14.7 %collective-permute-start = (f32[8,72,1]{2,1,0:T(8,128)}, f32[8,72,1]{2,1,0:T(8,128)}, u32[]{:S(2)}, u32[]{:S(2)}) collective-permute-start(f32[8,72,1]{2,1,0:T(8,128)} %get-tuple-element.163), channel_id=1, source_target_pairs={{1,0},{2,1},{3,2},{0,3},{5,4},{6,5},{7,6},{4,7},{9,8},{10,9},{11,1... | collective-permute-start | bytes 6920 | tf_op jit(solution)/shard_map/ppermute | solution.py:28
  122.5 5.2 copy-start.13
  122.5 5.2 copy-start.14
  122.5 46.4 %all-to-all-start.1 = ((f32[8,8,18,720]{3,0,2,1:T(8,128)}), f32[8,8,18,720]{3,0,2,1:T(8,128)}, u32[]{:S(2)}, u32[]{:S(2)}) async-start(f32[8,8,18,720]{3,0,2,1:T(8,128)} %copy.69), calls=%async_computation.1 | async-start | bytes 7077888 | tf_op jit(solution)/shard_map/all_to_all | solution.py:95
  470.8 7.2 copy-start.3
  470.8 20.6 %copy-start.5 = (f32[8,72,720]{2,1,0:T(8,128)}, f32[8,72,720]{2,1,0:T(8,128)S(1)}, u32[]{:S(2)}) copy-start(f32[8,72,720]{2,1,0:T(8,128)S(1)} %get-tuple-element.142) | copy-start | bytes 4976644
  470.9 12.2 %collective-permute-start.9 = (f32[1,72,720]{2,1,0:T(8,128)S(1)}, f32[1,72,720]{2,1,0:T(8,128)S(1)}, u32[]{:S(2)}, u32[]{:S(2)}) collective-permute-start(f32[1,72,720]{2,1,0:T(8,128)S(1)} %get-tuple-element.159), channel_id=1, source_target_pairs={{0,4},{4,8},{8,12},{12,16},{16,20},{20,24},{24,28},{1,5},{5,9},{9,... | collective-permute-start | bytes 622088 | tf_op jit(solution)/shard_map/ppermute | solution.py:27
  474.1 9.0 collective-permute-start.8
  475.4 13.2 %collective-permute-start.7 = (f32[2,72,720]{2,1,0:T(8,128)S(1)}, f32[2,72,720]{2,1,0:T(8,128)S(1)}, u32[]{:S(2)}, u32[]{:S(2)}) collective-permute-start(f32[2,72,720]{2,1,0:T(8,128)S(1)} %pad_maximum_fusion.13), channel_id=1, source_target_pairs={{0,2},{2,0},{1,3},{3,1},{4,6},{6,4},{5,7},{7,5},{8,10},{10,8},{9,1... | collective-permute-start | bytes 1244168 | tf_op jit(solution)/shard_map/ppermute | solution.py:17
  476.0 15.2 %collective-permute-start.6 = (f32[8,72,1]{2,1,0:T(8,128)S(1)}, f32[8,72,1]{2,1,0:T(8,128)S(1)}, u32[]{:S(2)}, u32[]{:S(2)}) collective-permute-start(f32[8,72,1]{2,1,0:T(8,128)S(1)} %get-tuple-element.162), channel_id=1, source_target_pairs={{0,1},{1,2},{2,3},{3,0},{4,5},{5,6},{6,7},{7,4},{8,9},{9,10},{10,1... | collective-permute-start | bytes 6920 | tf_op jit(solution)/shard_map/ppermute | solution.py:27
  476.1 15.3 %collective-permute-start.5 = (f32[8,72,1]{2,1,0:T(8,128)S(1)}, f32[8,72,1]{2,1,0:T(8,128)S(1)}, u32[]{:S(2)}, u32[]{:S(2)}) collective-permute-start(f32[8,72,1]{2,1,0:T(8,128)S(1)} %get-tuple-element.161), channel_id=1, source_target_pairs={{1,0},{2,1},{3,2},{0,3},{5,4},{6,5},{7,6},{4,7},{9,8},{10,9},{11,1... | collective-permute-start | bytes 6920 | tf_op jit(solution)/shard_map/ppermute | solution.py:28
  477.8 13.6 %copy-start.2 = (f32[8,72,720]{2,1,0:T(8,128)S(1)}, f32[8,72,720]{2,1,0:T(8,128)}, u32[]{:S(2)}) copy-start(f32[8,72,720]{2,1,0:T(8,128)} %param.21) | copy-start | bytes 4976644
  494.0 26.3 %collective-permute-start.14 = (f32[1,72,720]{2,1,0:T(8,128)S(1)}, f32[1,72,720]{2,1,0:T(8,128)S(1)}, u32[]{:S(2)}, u32[]{:S(2)}) collective-permute-start(f32[1,72,720]{2,1,0:T(8,128)S(1)} %get-tuple-element.155), channel_id=1, source_target_pairs={{0,4},{4,8},{8,12},{12,16},{16,20},{20,24},{24,28},{1,5},{5,9},{9,... | collective-permute-start | bytes 622088 | tf_op jit(solution)/shard_map/ppermute | solution.py:27
  498.3 22.0 %collective-permute-start.13 = (f32[1,72,720]{2,1,0:T(8,128)S(1)}, f32[1,72,720]{2,1,0:T(8,128)S(1)}, u32[]{:S(2)}, u32[]{:S(2)}) collective-permute-start(f32[1,72,720]{2,1,0:T(8,128)S(1)} %get-tuple-element.156), channel_id=1, source_target_pairs={{4,0},{8,4},{12,8},{16,12},{20,16},{24,20},{28,24},{5,1},{9,5},{13... | collective-permute-start | bytes 622088 | tf_op jit(solution)/shard_map/ppermute | solution.py:28
  499.8 20.5 %collective-permute-start.12 = (f32[2,72,720]{2,1,0:T(8,128)S(1)}, f32[2,72,720]{2,1,0:T(8,128)S(1)}, u32[]{:S(2)}, u32[]{:S(2)}) collective-permute-start(f32[2,72,720]{2,1,0:T(8,128)S(1)} %pad_maximum_fusion.14), channel_id=1, source_target_pairs={{0,2},{2,0},{1,3},{3,1},{4,6},{6,4},{5,7},{7,5},{8,10},{10,8},{9,1... | collective-permute-start | bytes 1244168 | tf_op jit(solution)/shard_map/ppermute | solution.py:17
  501.1 18.1 %collective-permute-start.11 = (f32[8,72,1]{2,1,0:T(8,128)S(1)}, f32[8,72,1]{2,1,0:T(8,128)S(1)}, u32[]{:S(2)}, u32[]{:S(2)}) collective-permute-start(f32[8,72,1]{2,1,0:T(8,128)S(1)} %get-tuple-element.152), channel_id=1, source_target_pairs={{0,1},{1,2},{2,3},{3,0},{4,5},{5,6},{6,7},{7,4},{8,9},{9,10},{10,1... | collective-permute-start | bytes 6920 | tf_op jit(solution)/shard_map/ppermute | solution.py:27
  501.6 17.6 %collective-permute-start.10 = (f32[8,72,1]{2,1,0:T(8,128)S(1)}, f32[8,72,1]{2,1,0:T(8,128)S(1)}, u32[]{:S(2)}, u32[]{:S(2)}) collective-permute-start(f32[8,72,1]{2,1,0:T(8,128)S(1)} %get-tuple-element.151), channel_id=1, source_target_pairs={{1,0},{2,1},{3,2},{0,3},{5,4},{6,5},{7,6},{4,7},{9,8},{10,9},{11,1... | collective-permute-start | bytes 6920 | tf_op jit(solution)/shard_map/ppermute | solution.py:28
  612.0 46.0 %all-to-all-start.5 = ((f32[8,8,18,720]{3,0,2,1:T(8,128)}), f32[8,8,18,720]{3,0,2,1:T(8,128)}, u32[]{:S(2)}, u32[]{:S(2)}) async-start(f32[8,8,18,720]{3,0,2,1:T(8,128)} %copy.82), calls=%async_computation.5 | async-start | bytes 7077888 | tf_op jit(solution)/shard_map/all_to_all | solution.py:95
  964.6 7.4 copy-start.7
  964.6 20.7 %copy-start.8 = (f32[8,72,720]{2,1,0:T(8,128)}, f32[8,72,720]{2,1,0:T(8,128)S(1)}, u32[]{:S(2)}) copy-start(f32[8,72,720]{2,1,0:T(8,128)S(1)} %get-tuple-element.138) | copy-start | bytes 4976644
  964.6 12.4 %collective-permute-start.19 = (f32[1,72,720]{2,1,0:T(8,128)S(1)}, f32[1,72,720]{2,1,0:T(8,128)S(1)}, u32[]{:S(2)}, u32[]{:S(2)}) collective-permute-start(f32[1,72,720]{2,1,0:T(8,128)S(1)} %get-tuple-element.147), channel_id=1, source_target_pairs={{0,4},{4,8},{8,12},{12,16},{16,20},{20,24},{24,28},{1,5},{5,9},{9,... | collective-permute-start | bytes 622088 | tf_op jit(solution)/shard_map/ppermute | solution.py:27
  968.1 9.0 collective-permute-start.18
  969.4 13.2 %collective-permute-start.17 = (f32[2,72,720]{2,1,0:T(8,128)S(1)}, f32[2,72,720]{2,1,0:T(8,128)S(1)}, u32[]{:S(2)}, u32[]{:S(2)}) collective-permute-start(f32[2,72,720]{2,1,0:T(8,128)S(1)} %pad_maximum_fusion.15), channel_id=1, source_target_pairs={{0,2},{2,0},{1,3},{3,1},{4,6},{6,4},{5,7},{7,5},{8,10},{10,8},{9,1... | collective-permute-start | bytes 1244168 | tf_op jit(solution)/shard_map/ppermute | solution.py:17
  969.9 15.2 %collective-permute-start.16 = (f32[8,72,1]{2,1,0:T(8,128)S(1)}, f32[8,72,1]{2,1,0:T(8,128)S(1)}, u32[]{:S(2)}, u32[]{:S(2)}) collective-permute-start(f32[8,72,1]{2,1,0:T(8,128)S(1)} %get-tuple-element.150), channel_id=1, source_target_pairs={{0,1},{1,2},{2,3},{3,0},{4,5},{5,6},{6,7},{7,4},{8,9},{9,10},{10,1... | collective-permute-start | bytes 6920 | tf_op jit(solution)/shard_map/ppermute | solution.py:27
  970.0 15.3 %collective-permute-start.15 = (f32[8,72,1]{2,1,0:T(8,128)S(1)}, f32[8,72,1]{2,1,0:T(8,128)S(1)}, u32[]{:S(2)}, u32[]{:S(2)}) collective-permute-start(f32[8,72,1]{2,1,0:T(8,128)S(1)} %get-tuple-element.149), channel_id=1, source_target_pairs={{1,0},{2,1},{3,2},{0,3},{5,4},{6,5},{7,6},{4,7},{9,8},{10,9},{11,1... | collective-permute-start | bytes 6920 | tf_op jit(solution)/shard_map/ppermute | solution.py:28
  (6 other events, 18.5 us)
where the time goes:
time: 1000 us; the launch traced here: 989 us
  blocking collectives  477 us (48%)
  local copies, waits for them, and re-layouts  268 us (27%)
  waiting for transfers between devices  136 us (14%)
  matrix products  52.8 us (5%)
  starting transfers between devices  42.3 us (4%)
  other arithmetic  11.1 us (1%)
    all_to_all x2, blocking collectives, polar_filter(): lax.all_to_all(sectioned, 'lat', split_axis=2, concat_axis=0, tiled=True)  172 us
    all_to_all x2, blocking collectives, polar_filter(): lax.all_to_all(spread, 'lat', split_axis=0, concat_axis=2, tiled=True)  159 us
    all_to_all x2, blocking collectives, polar_filter(): lax.all_to_all(lax.all_to_all(spread, 'lat', split_axis=0, concat_axis=2,...  146 us
    all_to_all x2, waiting for transfers between devices, polar_filter(): lax.all_to_all(lax.all_to_all(sectioned, 'lat', split_axis=2, concat_axis...  82.1 us
    another operation x16, local copies, waits for them, and re-layouts, toeplitz(): tiled = jnp.tile(padded, outputs)[:outputs * (outputs + tap_count)]  65.7 us
    dot_general x8, matrix products, one_row(): jnp.einsum('vbk,ok->vbo', window_row, matrix, precision=lax.Precision.HIG...  46.4 us
    reshape x8, local copies, waits for them, and re-layouts, toeplitz(): return tiled.reshape(outputs, outputs + tap_count)  46.1 us
    ppermute x8, waiting for transfers between devices, extended(): before = lax.ppermute(last, axis, up)  42 us
  transfers between devices with their start and end apart: 22, of which 13 were waited for; matrix products, arithmetic and copies ran while one was open for 1% of the time, Pallas kernels for 0%

commit v1 on v0

v1 whole, which is shorter than its diff:
```python
import jax
import jax.numpy as jnp
from jax import lax
from jax.sharding import PartitionSpec as P

meridional = 0.5
compress = 0.5
BLOCK = 256


def kernels(kernel_taps, filter_width):
    tap_count = kernel_taps.shape[1]
    offsets = jnp.abs(jnp.arange(tap_count, dtype=jnp.int32) - tap_count // 2)
    kept_taps = jnp.where(
        offsets[None, :] <= filter_width[:, None], kernel_taps, jnp.zeros_like(kernel_taps)
    )
    return kept_taps / jnp.sum(kept_taps, axis=1, keepdims=True)


def toeplitz(weights, outputs):
    rows, taps = weights.shape
    padded = jnp.concatenate([weights, jnp.zeros((rows, outputs + 1), weights.dtype)], axis=1)
    tiled = jnp.tile(padded, (1, outputs))[:, : outputs * (outputs + taps)]
    return tiled.reshape(rows, outputs, outputs + taps)


def pole_rows(values, sign_flip):
    lat_index, lat_count = lax.axis_index("lat"), lax.axis_size("lat")
    lon_count = lax.axis_size("lon")
    up = [(i, i + 1) for i in range(lat_count - 1)]
    south = lax.ppermute(values[-1], "lat", up)
    north = lax.ppermute(values[0], "lat", [(j, i) for i, j in up])
    route = []
    for lat in (0, lat_count - 1):
        for lon in range(lon_count):
            route.append((lat * lon_count + lon, lat * lon_count + (lon + lon_count // 2) % lon_count))
    edge = jnp.where(lat_index == 0, values[0], values[-1])
    partner = sign_flip * lax.ppermute(edge, ("lat", "lon"), route)
    south = jnp.where(lat_index == 0, partner, south)
    north = jnp.where(lat_index == lat_count - 1, partner, north)
    return south[None], north[None]


def lon_sides(values, width):
    count = lax.axis_size("lon")
    up = [(i, (i + 1) % count) for i in range(count)]
    before = lax.ppermute(values[..., -width:], "lon", up)
    after = lax.ppermute(values[..., :width], "lon", [(j, i) for i, j in up])
    return before, after


def on_device(zonal, merid, pressure, zonal_metric, helm_inverse, kernel_taps, filter_width):
    rows, levels, cols = pressure.shape
    taps = kernel_taps.shape[1]
    half = taps // 2
    lat_index, lat_count = lax.axis_index("lat"), lax.axis_size("lat")
    polar = (lat_index == 0) | (lat_index == lat_count - 1)
    weights = kernels(kernel_taps, filter_width)
    weights = jnp.where(lat_index == 0, weights[:rows], weights[rows:])
    band = toeplitz(weights, BLOCK)
    blocks = -(-cols // BLOCK)
    metric = zonal_metric[:, None, None]
    for step_index in range(2):
        south, north = pole_rows(pressure, 1.0)
        tall = jnp.concatenate([south, pressure, north], axis=0)
        before, after = lon_sides(tall, half + 1)
        wide = jnp.concatenate([before, tall, after], axis=2)
        tend_u = -metric * 0.5 * (wide[1:-1, :, 2:] - wide[1:-1, :, :-2])
        tend_v = -meridional * 0.5 * (wide[2:, :, 1:-1] - wide[:-2, :, 1:-1])
        tendency = jnp.concatenate([tend_u, tend_v], axis=1)
        padded = jnp.pad(tendency, ((0, 0), (0, 0), (0, blocks * BLOCK - cols)))
        windows = jnp.stack(
            [padded[..., b * BLOCK : b * BLOCK + BLOCK + taps] for b in range(blocks)], axis=1
        )
        smooth = jnp.einsum("rbvk,rok->rvbo", windows, band, precision=lax.Precision.HIGH)
        smooth = smooth.reshape(rows, 2 * levels, blocks * BLOCK)[..., :cols]
        smooth = jnp.where(polar, smooth, tendency[..., half : half + cols])
        zonal = zonal + smooth[:, :levels]
        merid = merid + smooth[:, levels:]
        south, north = pole_rows(merid, -1.0)
        before, after = lon_sides(zonal, 1)
        wide = jnp.concatenate([before, zonal, after], axis=2)
        tall = jnp.concatenate([south, merid, north], axis=0)
        divergence = metric * 0.5 * (wide[..., 2:] - wide[..., :-2]) + meridional * 0.5 * (
            tall[2:] - tall[:-2]
        )
        source = pressure - compress * divergence
        pressure = jnp.einsum(
            "rkl,rlc->rkc", helm_inverse, source, precision=lax.Precision.HIGH
        )
    return (zonal, merid, pressure)


def solution(mesh):
    field = P("lat", None, "lon")
    return jax.shard_map(
        on_device,
        mesh=mesh,
        in_specs=(field, field, field, P("lat"), P("lat", None, None), P(), P()),
        out_specs=(field, field, field),
        check_vma=False,
    )
```

time: 1000 us -> 198 us (0.20); the launches traced: 989 us -> 197 us
  blocking collectives: 477 us -> 0 us
  local copies, waits for them, and re-layouts: 268 us -> 42.6 us
  waiting for transfers between devices: 136 us -> 65.7 us
  matrix products: 52.8 us -> 26.1 us
  other arithmetic: 11.1 us -> 28.5 us
    all_to_all x6 -> x0, blocking collectives: 477 us -> none  [the longest x2 172 us: polar_filter(): lax.all_to_all(sectioned, 'lat', split_axis=2, concat_axis=0, tiled=True)]
    all_to_all x14 -> x0, local copies, waits for them, and re-layouts: 90.9 us -> none  [the longest x6 34.9 us: polar_filter(): lax.all_to_all(lax.all_to_all(sectioned, 'lat', split_axis=2, concat_axis...]
    all_to_all x2 -> x0, waiting for transfers between devices: 82.1 us -> none  [polar_filter(): lax.all_to_all(lax.all_to_all(sectioned, 'lat', split_axis=2, concat_axis...]
    another operation x26 -> x4, local copies, waits for them, and re-layouts: 70.8 us -> 16.9 us  [the longest x2 12.7 us: toeplitz(): tiled = jnp.tile(padded, (1, outputs))[:, :outputs * (outputs + taps)]]
    reshape x10 -> x2, local copies, waits for them, and re-layouts: 50.2 us -> 4.54 us  [on_device(): smooth = smooth.reshape(rows, 2 * levels, blocks * BLOCK)[..., :cols]]
    scatter x6 -> x0, local copies, waits for them, and re-layouts: 41.6 us -> none  [polar_filter(): spread.at[0].set(filtered[:row_share]).at[-1].set(filtered[row_share:])]
    dot_general x8 -> x2, matrix products: 46.4 us -> 21.2 us  [on_device(): jnp.einsum('rbvk,rok->rvbo', windows, band, precision=lax.Precision.HIGH)]
    ppermute x20, waiting for transfers between devices: 53.8 us -> 65.7 us  [the longest x4 31.2 us: lon_sides(): after = lax.ppermute(values[..., :width], 'lon', [(j, i) for i, j in up])]
  transfers between devices with their start and end apart: 22 -> 20, of which waited for: 13 -> 17; matrix products, arithmetic and copies ran while one was open for 1% -> 10% of each run, Pallas kernels for 0% -> 0%
where the time goes in v1:
time: 198 us; the launch traced here: 197 us
  waiting for transfers between devices  65.7 us (33%)
  local copies, waits for them, and re-layouts  42.6 us (22%)
  starting transfers between devices  33.5 us (17%)
  other arithmetic  28.5 us (14%)
  matrix products  26.1 us (13%)
    ppermute x4, waiting for transfers between devices, lon_sides(): after = lax.ppermute(values[..., :width], 'lon', [(j, i) for i, j in up])  31.2 us
    dot_general x2, matrix products, on_device(): jnp.einsum('rbvk,rok->rvbo', windows, band, precision=lax.Precision.HIGH)  21.2 us
    ppermute x4, waiting for transfers between devices, pole_rows(): south = lax.ppermute(values[-1], 'lat', up)  19 us
    ppermute x4, starting transfers between devices, pole_rows(): partner = sign_flip * lax.ppermute(edge, ('lat', 'lon'), route)  14.2 us
    mul x2, other arithmetic, on_device(): tend_v = -meridional * 0.5 * (wide[2:, :, 1:-1] - wide[:-2, :, 1:-1])  14.1 us
    another operation x2, local copies, waits for them, and re-layouts, toeplitz(): tiled = jnp.tile(padded, (1, outputs))[:, :outputs * (outputs + taps)]  12.7 us
    ppermute x4, starting transfers between devices, pole_rows(): south = lax.ppermute(values[-1], 'lat', up)  11.7 us
    concatenate x2, local copies, waits for them, and re-layouts, on_device(): wide = jnp.concatenate([before, tall, after], axis=2)  9.14 us
  transfers between devices with their start and end apart: 20, of which 17 were waited for; matrix products, arithmetic and copies ran while one was open for 10% of the time, Pallas kernels for 0%

profile of v1, /device:TPU:0, one launch (start us, length us, event | category | flops | bytes accessed | tf_op | source)
XLA Modules:
  0.0 197.5 jit_solution(5019917878357727600)
XLA Ops:
  1.8 4.9 %collective-permute-start = (f32[72,720]{1,0:T(8,128)S(1)}, f32[72,720]{1,0:T(8,128)S(1)}, u32[]{:S(2)}, u32[]{:S(2)}) collective-permute-start(f32[72,720]{1,0:T(8,128)S(1)} %broadcast_select_fusion.3), channel_id=1, source_target_pairs={{0,2},{1,3},{2,0},{3,1},{28,30},{29,31},{30,28},{31,29}} | collective-permute-start | bytes 622088 | tf_op jit(solution)/shard_map/ppermute | solution.py:38
  12.1 6.4 %collective-permute-done.1 = f32[72,720]{1,0:T(8,128)S(1)} collective-permute-done((f32[72,720]{1,0:T(8,128)S(1)}, f32[72,720]{1,0:T(8,128)S(1)}, u32[]{:S(2)}, u32[]{:S(2)}) %collective-permute-start.1) | collective-permute-done | bytes 207392 | tf_op jit(solution)/shard_map/ppermute | solution.py:31
  22.7 3.4 %tile.4 = f32[8,256,769]{2,1,0:T(8,128)} broadcast(f32[8,769]{1,0:T(8,128)S(1)} %concatenate.49), dimensions={0,2} | broadcast | bytes 6324256 | tf_op jit(solution)/shard_map/tile | solution.py:23
  26.1 9.3 %tile.10 = f32[8,196864]{1,0:T(8,128)} reshape(f32[8,256,769]{2,1,0:T(8,128)} %tile.4) | data formatting | bytes 12599296 | tf_op jit(solution)/shard_map/tile | solution.py:23
  35.4 4.8 %slice.218 = f32[8,196608]{1,0:T(8,128)} slice(f32[8,196864]{1,0:T(8,128)} %tile.10), slice={[0:8], [0:196608]} | slice | bytes 12582912 | tf_op jit(solution)/shard_map/slice | solution.py:23
  40.2 6.5 %collective-permute-done.4 = f32[10,72,257]{2,1,0:T(8,128)} collective-permute-done((f32[10,72,257]{2,1,0:T(8,128)}, f32[10,72,257]{2,1,0:T(8,128)}, u32[]{:S(2)}, u32[]{:S(2)}) %collective-permute-start.4) | collective-permute-done | bytes 740192 | tf_op jit(solution)/shard_map/ppermute | solution.py:48
  48.3 4.6 %concatenate.51 = f32[10,72,1234]{2,1,0:T(8,128)} concatenate(f32[10,72,257]{2,1,0:T(8,128)} %collective-permute-done.3, f32[10,72,720]{2,1,0:T(8,128)S(1)} %pad_maximum_fusion.3, f32[10,72,257]{2,1,0:T(8,128)} %collective-permute-done.4), dimensions={2} | concatenate | bytes 7107840 | tf_op jit(solution)/shard_map/concatenate | solution.py:67
  52.9 7.0 %fusion.26 = (f32[8,72,1232]{2,1,0:T(8,128)S(1)}, f32[8,72,1232]{2,1,0:T(8,128)S(1)}) fusion(f32[10,72,1234]{2,1,0:T(8,128)} %concatenate.51, f32[8]{0:T(128)S(1)} %get-tuple-element.40), kind=kLoop, calls=%fused_computation.47 | loop fusion | flops 2838528 | bytes 17031200 | tf_op jit(solution)/shard_map/mul | solution.py:69
  60.5 3.8 %fusion.19 = (f32[8,1,144,768]{3,2,1,0:T(8,128)}, f32[8,1,144,768]{3,2,1,0:T(8,128)}) fusion(f32[8,72,1232]{2,1,0:T(8,128)S(1)} %get-tuple-element.10, f32[8,72,1232]{2,1,0:T(8,128)S(1)} %get-tuple-element.9), kind=kLoop, calls=%fused_computation.37 | loop fusion | flops 1769472 | bytes 12754944 | tf_op jit(solution)/shard_map/stack | solution.py:72
  64.3 2.1 %fusion.10 = f32[8,1,144,768]{3,2,1,0:T(8,128)} fusion(f32[8,144,1232]{2,1,0:T(8,128)S(1)} %pad_maximum_fusion.1), kind=kLoop, calls=%fused_computation.28 | loop fusion | bytes 9216000 | tf_op jit(solution)/shard_map/stack | solution.py:72
  66.4 11.7 %fusion.31 = f32[8,3,18,8,256]{4,3,2,1,0:T(8,128)} fusion(f32[8,1,144,768]{3,2,1,0:T(8,128)} %fusion.10, f32[8,1,144,768]{3,2,1,0:T(8,128)} %get-tuple-element.6, f32[8,1,144,768]{3,2,1,0:T(8,128)} %get-tuple-element.5, f32[1,8,256,768]{3,1,2,0:T(8,128)S(1)} %bitcast.99), kind=kOutput, calls=%fused_computation.53 | convolution fusion | flops 4082171904 | bytes 20447232 | tf_op jit(solution)/shard_map/rbvk,rok->rvbo/dot_general | solution.py:75
  78.2 2.3 %copy.21 = f32[8,3,18,8,256]{4,3,1,2,0:T(8,128)S(1)} copy(f32[8,3,18,8,256]{4,3,2,1,0:T(8,128)} %fusion.31) | data formatting | bytes 7077888 | tf_op jit(solution)/shard_map/reshape | solution.py:76
  83.0 3.3 %collective-permute-start.7 = (f32[72,720]{1,0:T(8,128)S(1)}, f32[72,720]{1,0:T(8,128)S(1)}, u32[]{:S(2)}, u32[]{:S(2)}) collective-permute-start(f32[72,720]{1,0:T(8,128)S(1)} %broadcast_select_fusion.2), channel_id=1, source_target_pairs={{0,2},{1,3},{2,0},{3,1},{28,30},{29,31},{30,28},{31,29}} | collective-permute-start | bytes 622088 | tf_op jit(solution)/shard_map/ppermute | solution.py:38
  87.6 4.6 %collective-permute-start.9 = (f32[72,720]{1,0:T(8,128)S(1)}, f32[72,720]{1,0:T(8,128)S(1)}, u32[]{:S(2)}, u32[]{:S(2)}) collective-permute-start(f32[72,720]{1,0:T(8,128)S(1)} %get-tuple-element.28), channel_id=1, source_target_pairs={{0,4},{4,8},{8,12},{12,16},{16,20},{20,24},{24,28},{1,5},{5,9},{9,... | collective-permute-start | bytes 622088 | tf_op jit(solution)/shard_map/ppermute | solution.py:31
  92.9 2.2 %collective-permute-done.8 = f32[72,720]{1,0:T(8,128)S(1)} collective-permute-done((f32[72,720]{1,0:T(8,128)S(1)}, f32[72,720]{1,0:T(8,128)S(1)}, u32[]{:S(2)}, u32[]{:S(2)}) %collective-permute-start.8) | collective-permute-done | bytes 207392 | tf_op jit(solution)/shard_map/ppermute | solution.py:32
  95.0 3.5 %collective-permute-done.9 = f32[72,720]{1,0:T(8,128)S(1)} collective-permute-done((f32[72,720]{1,0:T(8,128)S(1)}, f32[72,720]{1,0:T(8,128)S(1)}, u32[]{:S(2)}, u32[]{:S(2)}) %collective-permute-start.9) | collective-permute-done | bytes 207392 | tf_op jit(solution)/shard_map/ppermute | solution.py:31
  99.2 1.9 collective-permute-done.6
  103.0 3.0 %collective-permute-start.10 = (f32[72,720]{1,0:T(8,128)S(1)}, f32[72,720]{1,0:T(8,128)S(1)}, u32[]{:S(2)}, u32[]{:S(2)}) collective-permute-start(f32[72,720]{1,0:T(8,128)S(1)} %broadcast_select_fusion.1), channel_id=1, source_target_pairs={{0,2},{1,3},{2,0},{3,1},{28,30},{29,31},{30,28},{31,29}} | collective-permute-start | bytes 622088 | tf_op jit(solution)/shard_map/ppermute | solution.py:38
  108.7 2.9 %collective-permute-done.10 = f32[72,720]{1,0:T(8,128)S(1)} collective-permute-done((f32[72,720]{1,0:T(8,128)S(1)}, f32[72,720]{1,0:T(8,128)S(1)}, u32[]{:S(2)}, u32[]{:S(2)}) %collective-permute-start.10) | collective-permute-done | bytes 207392 | tf_op jit(solution)/shard_map/ppermute | solution.py:38
  111.6 5.0 %collective-permute-done.11 = f32[72,720]{1,0:T(8,128)S(1)} collective-permute-done((f32[72,720]{1,0:T(8,128)S(1)}, f32[72,720]{1,0:T(8,128)S(1)}, u32[]{:S(2)}, u32[]{:S(2)}) %collective-permute-start.11) | collective-permute-done | bytes 207392 | tf_op jit(solution)/shard_map/ppermute | solution.py:31
  117.7 23.6 %collective-permute-done.14 = f32[10,72,257]{2,1,0:T(8,128)S(1)} collective-permute-done((f32[10,72,257]{2,1,0:T(8,128)S(1)}, f32[10,72,257]{2,1,0:T(8,128)S(1)}, u32[]{:S(2)}, u32[]{:S(2)}) %collective-permute-start.14) | collective-permute-done | bytes 740192 | tf_op jit(solution)/shard_map/ppermute | solution.py:48
  143.8 4.6 %concatenate.58 = f32[10,72,1234]{2,1,0:T(8,128)} concatenate(f32[10,72,257]{2,1,0:T(8,128)} %collective-permute-done.13, f32[10,72,720]{2,1,0:T(8,128)S(1)} %pad_maximum_fusion.4, f32[10,72,257]{2,1,0:T(8,128)} %copy-done.12), dimensions={2} | concatenate | bytes 7107840 | tf_op jit(solution)/shard_map/concatenate | solution.py:67
  148.4 7.0 %fusion.24 = (f32[8,72,1232]{2,1,0:T(8,128)S(1)}, f32[8,72,1232]{2,1,0:T(8,128)S(1)}) fusion(f32[10,72,1234]{2,1,0:T(8,128)} %concatenate.58, f32[8]{0:T(128)S(1)} %get-tuple-element.40), kind=kLoop, calls=%fused_computation.43 | loop fusion | flops 2838528 | bytes 17031200 | tf_op jit(solution)/shard_map/mul | solution.py:69
  156.0 3.8 %fusion.13 = (f32[8,1,144,768]{3,2,0,1:T(8,128)}, f32[8,1,144,768]{3,2,0,1:T(8,128)}) fusion(f32[8,72,1232]{2,1,0:T(8,128)S(1)} %get-tuple-element.8, f32[8,72,1232]{2,1,0:T(8,128)S(1)} %get-tuple-element.7), kind=kLoop, calls=%fused_computation.31 | loop fusion | flops 1769472 | bytes 12754944 | tf_op jit(solution)/shard_map/stack | solution.py:72
  159.7 2.1 %fusion.11 = f32[8,1,144,768]{3,2,0,1:T(8,128)} fusion(f32[8,144,1232]{2,1,0:T(8,128)S(1)} %pad_maximum_fusion.2), kind=kLoop, calls=%fused_computation.29 | loop fusion | bytes 9216000 | tf_op jit(solution)/shard_map/stack | solution.py:72
  161.9 9.5 %fusion.28 = f32[8,3,18,8,256]{4,3,2,1,0:T(8,128)} fusion(f32[1,8,256,768]{3,1,2,0:T(8,128)S(1)} %bitcast.102, f32[8,1,144,768]{3,2,0,1:T(8,128)} %fusion.11, f32[8,1,144,768]{3,2,0,1:T(8,128)} %get-tuple-element.4, f32[8,1,144,768]{3,2,0,1:T(8,128)} %get-tuple-element.3), kind=kOutput, calls=%fused_computation.52 | convolution fusion | flops 4082171904 | bytes 20447232 | tf_op jit(solution)/shard_map/rbvk,rok->rvbo/dot_general | solution.py:75
  171.4 2.3 %copy.22 = f32[8,3,18,8,256]{4,3,1,2,0:T(8,128)S(1)} copy(f32[8,3,18,8,256]{4,3,2,1,0:T(8,128)} %fusion.28) | data formatting | bytes 7077888 | tf_op jit(solution)/shard_map/reshape | solution.py:76
  176.2 3.0 %collective-permute-start.17 = (f32[72,720]{1,0:T(8,128)S(1)}, f32[72,720]{1,0:T(8,128)S(1)}, u32[]{:S(2)}, u32[]{:S(2)}) collective-permute-start(f32[72,720]{1,0:T(8,128)S(1)} %broadcast_select_fusion), channel_id=1, source_target_pairs={{0,2},{1,3},{2,0},{3,1},{28,30},{29,31},{30,28},{31,29}} | collective-permute-start | bytes 622088 | tf_op jit(solution)/shard_map/ppermute | solution.py:38
  180.5 4.6 %collective-permute-start.19 = (f32[72,720]{1,0:T(8,128)S(1)}, f32[72,720]{1,0:T(8,128)S(1)}, u32[]{:S(2)}, u32[]{:S(2)}) collective-permute-start(f32[72,720]{1,0:T(8,128)S(1)} %get-tuple-element.22), channel_id=1, source_target_pairs={{0,4},{4,8},{8,12},{12,16},{16,20},{20,24},{24,28},{1,5},{5,9},{9,... | collective-permute-start | bytes 622088 | tf_op jit(solution)/shard_map/ppermute | solution.py:31
  186.5 2.2 %collective-permute-done.18 = f32[72,720]{1,0:T(8,128)S(1)} collective-permute-done((f32[72,720]{1,0:T(8,128)S(1)}, f32[72,720]{1,0:T(8,128)S(1)}, u32[]{:S(2)}, u32[]{:S(2)}) %collective-permute-start.18) | collective-permute-done | bytes 207392 | tf_op jit(solution)/shard_map/ppermute | solution.py:32
  188.7 4.2 %collective-permute-done.19 = f32[72,720]{1,0:T(8,128)S(1)} collective-permute-done((f32[72,720]{1,0:T(8,128)S(1)}, f32[72,720]{1,0:T(8,128)S(1)}, u32[]{:S(2)}, u32[]{:S(2)}) %collective-permute-start.19) | collective-permute-done | bytes 207392 | tf_op jit(solution)/shard_map/ppermute | solution.py:31
  194.5 3.0 %fusion.65 = f32[8,72,720]{2,1,0:T(8,128)} fusion(f32[8,72,72]{2,1,0:T(8,128)S(1)} %copy-done, f32[8,72,720]{2,1,0:T(8,128)S(1)} %copy-done.2, f32[8,72,720]{2,1,0:T(8,128)S(1)} %get-tuple-element.11, f32[1,72,720]{2,1,0:T(8,128)S(1)} %get-tuple-element.32, f32[1,72,720]{2,1,0:T(8,128)S(1)} %get-tuple-element.31, f32[8,72,720]{2,1,0:T(8,128)S(1)} %get-tuple-element.12, ...), kind=kOutput, calls=%fused_computation.91 | convolution fusion | flops 183720960 | bytes 7220768 | tf_op jit(solution)/shard_map/rkl,rlc->rkc/dot_general | solution.py:88
  (97 shorter events, 33.5 us)
Async XLA Ops:
  0.6 100.5 %copy-start = (f32[8,72,72]{2,1,0:T(8,128)S(1)}, f32[8,72,72]{2,1,0:T(8,128)}, u32[]{:S(2)}) copy-start(f32[8,72,72]{2,1,0:T(8,128)} %param.11) | copy-start | bytes 497668
  1.8 10.3 %collective-permute-start = (f32[72,720]{1,0:T(8,128)S(1)}, f32[72,720]{1,0:T(8,128)S(1)}, u32[]{:S(2)}, u32[]{:S(2)}) collective-permute-start(f32[72,720]{1,0:T(8,128)S(1)} %broadcast_select_fusion.3), channel_id=1, source_target_pairs={{0,2},{1,3},{2,0},{3,1},{28,30},{29,31},{30,28},{31,29}} | collective-permute-start | bytes 622088 | tf_op jit(solution)/shard_map/ppermute | solution.py:38
  7.7 10.7 %collective-permute-start.1 = (f32[72,720]{1,0:T(8,128)S(1)}, f32[72,720]{1,0:T(8,128)S(1)}, u32[]{:S(2)}, u32[]{:S(2)}) collective-permute-start(f32[72,720]{1,0:T(8,128)S(1)} %get-tuple-element.29), channel_id=1, source_target_pairs={{0,4},{4,8},{8,12},{12,16},{16,20},{20,24},{24,28},{1,5},{5,9},{9,... | collective-permute-start | bytes 622088 | tf_op jit(solution)/shard_map/ppermute | solution.py:31
  9.0 9.4 %collective-permute-start.2 = (f32[72,720]{1,0:T(8,128)S(1)}, f32[72,720]{1,0:T(8,128)S(1)}, u32[]{:S(2)}, u32[]{:S(2)}) collective-permute-start(f32[72,720]{1,0:T(8,128)S(1)} %get-tuple-element.30), channel_id=1, source_target_pairs={{4,0},{8,4},{12,8},{16,12},{20,16},{24,20},{28,24},{5,1},{9,5},{13... | collective-permute-start | bytes 622088 | tf_op jit(solution)/shard_map/ppermute | solution.py:32
  21.9 24.8 %collective-permute-start.4 = (f32[10,72,257]{2,1,0:T(8,128)}, f32[10,72,257]{2,1,0:T(8,128)}, u32[]{:S(2)}, u32[]{:S(2)}) collective-permute-start(f32[10,72,257]{2,1,0:T(8,128)} %get-tuple-element.17), channel_id=1, source_target_pairs={{1,0},{2,1},{3,2},{0,3},{5,4},{6,5},{7,6},{4,7},{9,8},{10,9},{11,1... | collective-permute-start | bytes 2220488 | tf_op jit(solution)/shard_map/ppermute | solution.py:48
  21.9 26.5 %collective-permute-start.3 = (f32[10,72,257]{2,1,0:T(8,128)}, f32[10,72,257]{2,1,0:T(8,128)}, u32[]{:S(2)}, u32[]{:S(2)}) collective-permute-start(f32[10,72,257]{2,1,0:T(8,128)} %get-tuple-element.18), channel_id=1, source_target_pairs={{0,1},{1,2},{2,3},{3,0},{4,5},{5,6},{6,7},{7,4},{8,9},{9,10},{10,1... | collective-permute-start | bytes 2220488 | tf_op jit(solution)/shard_map/ppermute | solution.py:47
  60.0 6.5 %slice-start = ((s8[6291456]{0:T(1024)(128)(4,1)}), s8[4194304]{0:T(1024)(128)(4,1)S(1)}, s32[]{:S(2)}) async-start(s8[6291456]{0:T(1024)(128)(4,1)} %bitcast.97), calls=%async_computation | async-start | bytes 8388608
  60.5 5.9 %slice-start.1 = ((s8[6291456]{0:T(1024)(128)(4,1)}), s8[2097152]{0:T(1024)(128)(4,1)S(1)}, s32[]{:S(2)}) async-start(s8[6291456]{0:T(1024)(128)(4,1)} %bitcast.97), calls=%async_computation.1 | async-start | bytes 4194304
  82.9 20.1 %copy-start.3 = (f32[8,72,720]{2,1,0:T(8,128)}, f32[8,72,720]{2,1,0:T(8,128)S(1)}, u32[]{:S(2)}) copy-start(f32[8,72,720]{2,1,0:T(8,128)S(1)} %get-tuple-element.13) | copy-start | bytes 4976644
  82.9 20.1 %copy-start.5 = (f32[8,72,720]{2,1,0:T(8,128)}, f32[8,72,720]{2,1,0:T(8,128)S(1)}, u32[]{:S(2)}) copy-start(f32[8,72,720]{2,1,0:T(8,128)S(1)} %get-tuple-element.14) | copy-start | bytes 4976644
  82.9 18.2 %copy-start.7 = (f32[8,72,720]{2,1,0:T(8,128)S(1)}, f32[8,72,720]{2,1,0:T(8,128)}, u32[]{:S(2)}) copy-start(f32[8,72,720]{2,1,0:T(8,128)} %param.9) | copy-start | bytes 4976644
  83.0 9.9 %collective-permute-start.7 = (f32[72,720]{1,0:T(8,128)S(1)}, f32[72,720]{1,0:T(8,128)S(1)}, u32[]{:S(2)}, u32[]{:S(2)}) collective-permute-start(f32[72,720]{1,0:T(8,128)S(1)} %broadcast_select_fusion.2), channel_id=1, source_target_pairs={{0,2},{1,3},{2,0},{3,1},{28,30},{29,31},{30,28},{31,29}} | collective-permute-start | bytes 622088 | tf_op jit(solution)/shard_map/ppermute | solution.py:38
  86.3 8.7 %collective-permute-start.8 = (f32[72,720]{1,0:T(8,128)S(1)}, f32[72,720]{1,0:T(8,128)S(1)}, u32[]{:S(2)}, u32[]{:S(2)}) collective-permute-start(f32[72,720]{1,0:T(8,128)S(1)} %get-tuple-element.27), channel_id=1, source_target_pairs={{4,0},{8,4},{12,8},{16,12},{20,16},{24,20},{28,24},{5,1},{9,5},{13... | collective-permute-start | bytes 622088 | tf_op jit(solution)/shard_map/ppermute | solution.py:32
  87.6 10.9 %collective-permute-start.9 = (f32[72,720]{1,0:T(8,128)S(1)}, f32[72,720]{1,0:T(8,128)S(1)}, u32[]{:S(2)}, u32[]{:S(2)}) collective-permute-start(f32[72,720]{1,0:T(8,128)S(1)} %get-tuple-element.28), channel_id=1, source_target_pairs={{0,4},{4,8},{8,12},{12,16},{16,20},{20,24},{24,28},{1,5},{5,9},{9,... | collective-permute-start | bytes 622088 | tf_op jit(solution)/shard_map/ppermute | solution.py:31
  92.3 6.9 %collective-permute-start.5 = (f32[8,72,1]{2,1,0:T(8,128)S(1)}, f32[8,72,1]{2,1,0:T(8,128)S(1)}, u32[]{:S(2)}, u32[]{:S(2)}) collective-permute-start(f32[8,72,1]{2,1,0:T(8,128)S(1)} %get-tuple-element.25), channel_id=1, source_target_pairs={{1,0},{2,1},{3,2},{0,3},{5,4},{6,5},{7,6},{4,7},{9,8},{10,9},{11,1... | collective-permute-start | bytes 6920 | tf_op jit(solution)/shard_map/ppermute | solution.py:48
  92.4 8.8 %collective-permute-start.6 = (f32[8,72,1]{2,1,0:T(8,128)S(1)}, f32[8,72,1]{2,1,0:T(8,128)S(1)}, u32[]{:S(2)}, u32[]{:S(2)}) collective-permute-start(f32[8,72,1]{2,1,0:T(8,128)S(1)} %get-tuple-element.26), channel_id=1, source_target_pairs={{0,1},{1,2},{2,3},{3,0},{4,5},{5,6},{6,7},{7,4},{8,9},{9,10},{10,1... | collective-permute-start | bytes 6920 | tf_op jit(solution)/shard_map/ppermute | solution.py:47
  103.0 13.8 %copy-start.1 = (f32[8,72,720]{2,1,0:T(8,128)}, f32[8,72,720]{2,1,0:T(8,128)S(1)}, u32[]{:S(2)}) copy-start(f32[8,72,720]{2,1,0:T(8,128)S(1)} %fusion.62) | copy-start | bytes 4976644
  103.0 8.5 %collective-permute-start.10 = (f32[72,720]{1,0:T(8,128)S(1)}, f32[72,720]{1,0:T(8,128)S(1)}, u32[]{:S(2)}, u32[]{:S(2)}) collective-permute-start(f32[72,720]{1,0:T(8,128)S(1)} %broadcast_select_fusion.1), channel_id=1, source_target_pairs={{0,2},{1,3},{2,0},{3,1},{28,30},{29,31},{30,28},{31,29}} | collective-permute-start | bytes 622088 | tf_op jit(solution)/shard_map/ppermute | solution.py:38
  106.1 10.5 %collective-permute-start.11 = (f32[72,720]{1,0:T(8,128)S(1)}, f32[72,720]{1,0:T(8,128)S(1)}, u32[]{:S(2)}, u32[]{:S(2)}) collective-permute-start(f32[72,720]{1,0:T(8,128)S(1)} %get-tuple-element.23), channel_id=1, source_target_pairs={{0,4},{4,8},{8,12},{12,16},{16,20},{20,24},{24,28},{1,5},{5,9},{9,... | collective-permute-start | bytes 622088 | tf_op jit(solution)/shard_map/ppermute | solution.py:31
  107.4 9.2 %collective-permute-start.12 = (f32[72,720]{1,0:T(8,128)S(1)}, f32[72,720]{1,0:T(8,128)S(1)}, u32[]{:S(2)}, u32[]{:S(2)}) collective-permute-start(f32[72,720]{1,0:T(8,128)S(1)} %get-tuple-element.24), channel_id=1, source_target_pairs={{4,0},{8,4},{12,8},{16,12},{20,16},{24,20},{28,24},{5,1},{9,5},{13... | collective-permute-start | bytes 622088 | tf_op jit(solution)/shard_map/ppermute | solution.py:32
  117.2 24.2 %collective-permute-start.14 = (f32[10,72,257]{2,1,0:T(8,128)S(1)}, f32[10,72,257]{2,1,0:T(8,128)S(1)}, u32[]{:S(2)}, u32[]{:S(2)}) collective-permute-start(f32[10,72,257]{2,1,0:T(8,128)S(1)} %get-tuple-element.15), channel_id=1, source_target_pairs={{1,0},{2,1},{3,2},{0,3},{5,4},{6,5},{7,6},{4,7},{9,8},{10,9},{11,1... | collective-permute-start | bytes 2220488 | tf_op jit(solution)/shard_map/ppermute | solution.py:48
  117.2 26.6 %collective-permute-start.13 = (f32[10,72,257]{2,1,0:T(8,128)S(1)}, f32[10,72,257]{2,1,0:T(8,128)}, u32[]{:S(2)}, u32[]{:S(2)}) collective-permute-start(f32[10,72,257]{2,1,0:T(8,128)S(1)} %get-tuple-element.16), channel_id=1, source_target_pairs={{0,1},{1,2},{2,3},{3,0},{4,5},{5,6},{6,7},{7,4},{8,9},{9,10},{10,1... | collective-permute-start | bytes 2220488 | tf_op jit(solution)/shard_map/ppermute | solution.py:47
  155.4 6.5 %slice-start.2 = ((s8[6291456]{0:T(1024)(128)(4,1)}), s8[4194304]{0:T(1024)(128)(4,1)S(1)}, s32[]{:S(2)}) async-start(s8[6291456]{0:T(1024)(128)(4,1)} %bitcast.100), calls=%async_computation.2 | async-start | bytes 8388608
  156.0 5.9 %slice-start.3 = ((s8[6291456]{0:T(1024)(128)(4,1)}), s8[2097152]{0:T(1024)(128)(4,1)S(1)}, s32[]{:S(2)}) async-start(s8[6291456]{0:T(1024)(128)(4,1)} %bitcast.100), calls=%async_computation.3 | async-start | bytes 4194304
  176.1 21.4 %copy-start.8 = (f32[8,72,720]{2,1,0:T(8,128)}, f32[8,72,720]{2,1,0:T(8,128)S(1)}, u32[]{:S(2)}) copy-start(f32[8,72,720]{2,1,0:T(8,128)S(1)} %get-tuple-element.11) | copy-start | bytes 4976644
  176.1 21.4 %copy-start.9 = (f32[8,72,720]{2,1,0:T(8,128)}, f32[8,72,720]{2,1,0:T(8,128)S(1)}, u32[]{:S(2)}) copy-start(f32[8,72,720]{2,1,0:T(8,128)S(1)} %get-tuple-element.12) | copy-start | bytes 4976644
  176.1 18.3 %copy-start.2 = (f32[8,72,720]{2,1,0:T(8,128)S(1)}, f32[8,72,720]{2,1,0:T(8,128)}, u32[]{:S(2)}) copy-start(f32[8,72,720]{2,1,0:T(8,128)} %copy-done.1) | copy-start | bytes 4976644
  176.2 10.3 %collective-permute-start.17 = (f32[72,720]{1,0:T(8,128)S(1)}, f32[72,720]{1,0:T(8,128)S(1)}, u32[]{:S(2)}, u32[]{:S(2)}) collective-permute-start(f32[72,720]{1,0:T(8,128)S(1)} %broadcast_select_fusion), channel_id=1, source_target_pairs={{0,2},{1,3},{2,0},{3,1},{28,30},{29,31},{30,28},{31,29}} | collective-permute-start | bytes 622088 | tf_op jit(solution)/shard_map/ppermute | solution.py:38
  179.2 9.5 %collective-permute-start.18 = (f32[72,720]{1,0:T(8,128)S(1)}, f32[72,720]{1,0:T(8,128)S(1)}, u32[]{:S(2)}, u32[]{:S(2)}) collective-permute-start(f32[72,720]{1,0:T(8,128)S(1)} %get-tuple-element.21), channel_id=1, source_target_pairs={{4,0},{8,4},{12,8},{16,12},{20,16},{24,20},{28,24},{5,1},{9,5},{13... | collective-permute-start | bytes 622088 | tf_op jit(solution)/shard_map/ppermute | solution.py:32
  180.5 12.4 %collective-permute-start.19 = (f32[72,720]{1,0:T(8,128)S(1)}, f32[72,720]{1,0:T(8,128)S(1)}, u32[]{:S(2)}, u32[]{:S(2)}) collective-permute-start(f32[72,720]{1,0:T(8,128)S(1)} %get-tuple-element.22), channel_id=1, source_target_pairs={{0,4},{4,8},{8,12},{12,16},{16,20},{20,24},{24,28},{1,5},{5,9},{9,... | collective-permute-start | bytes 622088 | tf_op jit(solution)/shard_map/ppermute | solution.py:31
  185.2 8.3 %collective-permute-start.15 = (f32[8,72,1]{2,1,0:T(8,128)S(1)}, f32[8,72,1]{2,1,0:T(8,128)S(1)}, u32[]{:S(2)}, u32[]{:S(2)}) collective-permute-start(f32[8,72,1]{2,1,0:T(8,128)S(1)} %get-tuple-element.19), channel_id=1, source_target_pairs={{1,0},{2,1},{3,2},{0,3},{5,4},{6,5},{7,6},{4,7},{9,8},{10,9},{11,1... | collective-permute-start | bytes 6920 | tf_op jit(solution)/shard_map/ppermute | solution.py:48
  186.1 8.4 %collective-permute-start.16 = (f32[8,72,1]{2,1,0:T(8,128)S(1)}, f32[8,72,1]{2,1,0:T(8,128)S(1)}, u32[]{:S(2)}, u32[]{:S(2)}) collective-permute-start(f32[8,72,1]{2,1,0:T(8,128)S(1)} %get-tuple-element.20), channel_id=1, source_target_pairs={{0,1},{1,2},{2,3},{3,0},{4,5},{5,6},{6,7},{7,4},{8,9},{9,10},{10,1... | collective-permute-start | bytes 6920 | tf_op jit(solution)/shard_map/ppermute | solution.py:47
  (8 other events, 17.2 us)

commit v2 on v1

v2 whole, which is shorter than its diff:
```python
import functools

import jax
import jax.numpy as jnp
from jax import lax
from jax.experimental import pallas as pl
from jax.experimental.pallas import tpu as pltpu
from jax.sharding import PartitionSpec as P

meridional = 0.5
compress = 0.5
BLOCK = 256
MESH = pl.DeviceIdType.MESH
NT = (((1,), (1,)), ((), ()))
EXACT = lax.Precision.HIGHEST
SOUTH, NORTH, COL_E, COL_W, WIDE_W, WIDE_E, RIM_W0, RIM_E0, RIM_W9, RIM_E9 = range(10)


def kernels(kernel_taps, filter_width):
    tap_count = kernel_taps.shape[1]
    offsets = jnp.abs(jnp.arange(tap_count, dtype=jnp.int32) - tap_count // 2)
    kept_taps = jnp.where(
        offsets[None, :] <= filter_width[:, None], kernel_taps, jnp.zeros_like(kernel_taps)
    )
    return kept_taps / jnp.sum(kept_taps, axis=1, keepdims=True)


def split(value):
    high = value.astype(jnp.bfloat16)
    return high, (value - high.astype(jnp.float32)).astype(jnp.bfloat16)


def kernel(
    sizes, u_in, v_in, p_in, metric_ref, helm_ref, weight_ref, u_out, v_out, p_out,
    p_tall, v_tall, u_wide, west, east, stage, cols_e, cols_w, send_cols, band_h, band_l,
    send_sem, recv_sem,
):
    rows, levels, cols, half, lats, lons = sizes
    padded = -(-cols // 128) * 128
    lat, lon = lax.axis_index("lat"), lax.axis_index("lon")
    first, final = lat == 0, lat == lats - 1
    polar = jnp.logical_or(first, final)
    inner = jnp.logical_not(polar)
    beside = jnp.logical_or(lat == 1, lat == lats - 2)
    pole = jnp.where(lat == 1, 0, lats - 1)
    shift = lambda n: lax.rem(lon + n + lons, lons)
    across = lons // 2
    last_base = (cols // 128) * 128
    rem = cols - last_base

    barrier = pltpu.get_barrier_semaphore()

    def greet(device):
        pl.semaphore_signal(barrier, inc=1, device_id=device, device_id_type=MESH)

    greet((lat, shift(1)))
    greet((lat, shift(-1)))

    @pl.when(lat > 0)
    def _():
        greet((lat - 1, lon))

    @pl.when(lat < lats - 1)
    def _():
        greet((lat + 1, lon))

    @pl.when(polar)
    def _():
        inward = jnp.where(first, 1, lats - 2)
        greet((inward, shift(1)))
        greet((inward, shift(-1)))
        greet((lat, shift(across)))
        greet((lat, shift(across + 1)))
        greet((lat, shift(across - 1)))

    @pl.when(beside)
    def _():
        greet((pole, shift(1)))
        greet((pole, shift(-1)))

    def fill(r, carry):
        p_tall[0, r + 1, :, 0:cols] = p_in[r]
        return carry

    lax.fori_loop(0, rows, fill, 0)

    @pl.when(polar)
    def _():
        pl.semaphore_wait(barrier, 8)

    @pl.when(jnp.logical_and(inner, beside))
    def _():
        pl.semaphore_wait(barrier, 6)

    @pl.when(jnp.logical_and(inner, jnp.logical_not(beside)))
    def _():
        pl.semaphore_wait(barrier, 4)

    def copy(phase, kind, src, dst, device):
        return pltpu.make_async_remote_copy(
            src_ref=src, dst_ref=dst, send_sem=send_sem.at[phase, kind],
            recv_sem=recv_sem.at[phase, kind], device_id=device, device_id_type=MESH,
        )


    def tall_rows(phase, tall, act):
        up = copy(phase, SOUTH, tall.at[rows], tall.at[0], (lat + 1, lon))
        down = copy(phase, NORTH, tall.at[1], tall.at[rows + 1], (lat - 1, lon))
        over0 = copy(phase, RIM_W0 + 4, tall.at[1], tall.at[0], (lat, shift(across)))
        over9 = copy(phase, RIM_W0 + 4, tall.at[rows], tall.at[rows + 1], (lat, shift(across)))
        if act == "start":
            pl.when(first)(over0.start)
            pl.when(final)(over9.start)
            pl.when(lat < lats - 1)(up.start)
            pl.when(lat > 0)(down.start)
        elif act == "recv":
            pl.when(first)(over0.wait_recv)
            pl.when(final)(over9.wait_recv)
            pl.when(lat > 0)(up.wait_recv)
            pl.when(lat < lats - 1)(down.wait_recv)
        else:
            pl.when(first)(over0.wait_send)
            pl.when(final)(over9.wait_send)
            pl.when(lat < lats - 1)(up.wait_send)
            pl.when(lat > 0)(down.wait_send)

    def columns(phase, act):
        down = copy(phase, COL_E, send_cols.at[phase, 0], cols_e.at[phase], (lat, shift(-1)))
        up = copy(phase, COL_W, send_cols.at[phase, 1], cols_w.at[phase], (lat, shift(1)))
        for one in (down, up):
            if act == "start":
                one.start()
            elif act == "recv":
                one.wait_recv()
            else:
                one.wait_send()

    def wide_sides(step, act):
        phase = 2 * step
        tall = p_tall.at[step]
        side = stage.at[step]

        @pl.when(polar)
        def _():
            up = copy(phase, WIDE_W, side, west.at[step, pl.ds(1, rows)], (lat, shift(1)))
            down = copy(
                phase, WIDE_E, tall.at[pl.ds(1, rows), :, pl.ds(0, half)],
                east.at[step, pl.ds(1, rows)], (lat, shift(-1)),
            )
            for one in (up, down):
                if act == "start":
                    one.start()
                elif act == "recv":
                    one.wait_recv()
                else:
                    one.wait_send()

        def rims(row, slot, kind, lat_to, lon_w, lon_e):
            to_west = copy(
                phase, kind, side.at[row], west.at[step, slot], (lat_to, lon_w)
            )
            to_east = copy(
                phase, kind + 1, tall.at[row + 1, :, pl.ds(0, half)],
                east.at[step, slot], (lat_to, lon_e),
            )
            return to_west, to_east

        def run(pair):
            for one in pair:
                if act == "start":
                    one.start()
                elif act == "recv":
                    one.wait_recv()
                else:
                    one.wait_send()

        own0 = rims(0, 0, RIM_W0, lat, shift(1 - across), shift(-1 - across))
        own9 = rims(rows - 1, rows + 1, RIM_W9, lat, shift(1 - across), shift(-1 - across))
        to_first = rims(0, rows + 1, RIM_W9, 0, shift(1), shift(-1))
        to_final = rims(rows - 1, 0, RIM_W0, lats - 1, shift(1), shift(-1))
        if act == "recv":
            @pl.when(polar)
            def _():
                run(own0)
                run(own9)
        else:
            pl.when(first)(lambda: run(own0))
            pl.when(final)(lambda: run(own9))
            pl.when(lat == 1)(lambda: run(to_first))
            pl.when(lat == lats - 2)(lambda: run(to_final))

    lane = lax.broadcasted_iota(jnp.int32, (rows, 128), 1)
    sub = lax.broadcasted_iota(jnp.int32, (rows, 128), 0)
    lane_l = lax.broadcasted_iota(jnp.int32, (levels, 128), 1)

    def column_of(tile_of, at):
        total = jnp.zeros((rows, levels), jnp.float32)
        base = (at // 128) * 128
        for r in range(rows):
            pick = jnp.where(jnp.logical_and(lane == at - base, sub == r), 1.0, 0.0)
            tile = tile_of(r, base)
            if base == last_base:
                tile = jnp.where(lane_l < rem, tile, 0.0)
            total += lax.dot_general(
                pick, tile, NT, precision=EXACT, preferred_element_type=jnp.float32
            )
        return total

    eye = jnp.where(
        lax.broadcasted_iota(jnp.int32, (levels, levels), 0)
        == lax.broadcasted_iota(jnp.int32, (levels, levels), 1),
        1.0, 0.0,
    )
    row_lane = lax.broadcasted_iota(jnp.int32, (levels, rows), 1)

    def upright(block):
        return lax.dot_general(
            eye, block, NT, precision=EXACT, preferred_element_type=jnp.float32
        )

    def take(stood, r):
        return jnp.sum(jnp.where(row_lane == r, stood, 0.0), axis=1, keepdims=True)

    lane_p = lax.broadcasted_iota(jnp.int32, (levels, padded), 1)
    blocks = -(-cols // BLOCK)
    window = blocks * BLOCK + 2 * half
    lane_w = lax.broadcasted_iota(jnp.int32, (levels, window), 1)
    lane_t = lax.broadcasted_iota(jnp.int32, (levels, half + 128), 1)

    def lon_difference(value, before, after):
        right = jnp.where(lane_p == cols - 1, after, pltpu.roll(value, padded - 1, 1))
        left = jnp.where(lane_p == 0, before, pltpu.roll(value, 1, 1))
        return 0.5 * (right - left)

    def wide_row(step, r):
        own = p_tall[step, r]
        tail = jnp.concatenate(
            [own[:, last_base:padded], jnp.zeros((levels, half), jnp.float32)], axis=1
        )
        moved = jnp.concatenate(
            [east[step, r], jnp.zeros((levels, 128), jnp.float32)], axis=1
        )
        tail = jnp.where(lane_t < rem, tail, pltpu.roll(moved, rem, 1))
        pieces = [west[step, r], own[:, 0:last_base], tail]
        rest = window - half - last_base - half - 128
        if rest:
            pieces.append(jnp.zeros((levels, rest), jnp.float32))
        return jnp.concatenate(pieces, axis=1)

    def send_pressure(step):
        phase = 2 * step
        tall_rows(phase, p_tall.at[step], "start")

        @pl.when(jnp.logical_or(polar, beside))
        def _():
            def edge(r, carry):
                value = p_tall[step, r + 1, :, padded - half - 128 : padded]
                turned = pltpu.roll(value, (half + 128) - (128 - (padded - cols)), 1)
                stage[step, r] = turned[:, 0:half]
                return carry

            lax.fori_loop(0, rows, edge, 0)

        wide_sides(step, "start")
        tile_of = lambda r, base: p_tall[step, r + 1, :, base : base + 128]
        send_cols[phase, 0] = column_of(tile_of, 0)

        @pl.when(polar)
        def _():
            send_cols[phase, 1] = column_of(tile_of, cols - half - 1)

        @pl.when(inner)
        def _():
            send_cols[phase, 1] = column_of(tile_of, cols - 1)

        columns(phase, "start")

    def store_winds(step, r, add_u, add_v, base, width):
        at = slice(base, base + width)
        if step == 0:
            u_wide[r, :, at] = u_in[r, :, at] + add_u
            v_tall[0, r + 1, :, at] = v_in[r, :, at] + add_v
        else:
            u_out[r, :, at] = u_wide[r, :, at] + add_u
            v_tall[1, r + 1, :, at] = v_tall[0, r + 1, :, at] + add_v

    for step in range(2):
        phase = 2 * step
        send_pressure(step)
        if step == 0:
            @pl.when(polar)
            def _():
                def build(r, carry):
                    line = jnp.broadcast_to(
                        weight_ref[pl.ds(r, 1), :], (BLOCK, 2 * half + BLOCK)
                    )
                    matrix = pltpu.roll(line, 0, 1, stride=1, stride_axis=0)
                    band_h[r], band_l[r] = split(matrix)
                    return carry

                lax.fori_loop(0, rows, build, 0)

        tall_rows(phase, p_tall.at[step], "recv")
        columns(phase, "recv")

        @pl.when(polar)
        def _():
            wide_sides(step, "recv")
            far = upright(cols_w[phase])

            def smooth(r, carry):
                scale = -0.5 * metric_ref[r]
                own = wide_row(step, r + 1)
                left = jnp.where(lane_w == 0, take(far, r), pltpu.roll(own, 1, 1))
                tend_u = scale * (pltpu.roll(own, window - 1, 1) - left)
                tend_v = (-meridional * 0.5) * (wide_row(step, r + 2) - wide_row(step, r))
                high, low = split(jnp.concatenate([tend_u, tend_v], axis=0))
                span = BLOCK + 2 * half
                highs = [high[:, b * BLOCK : b * BLOCK + span] for b in range(blocks)]
                lows = [low[:, b * BLOCK : b * BLOCK + span] for b in range(blocks)]
                main = lax.dot_general(
                    jnp.concatenate(highs + lows, axis=0), band_h[r], NT,
                    preferred_element_type=jnp.float32,
                )
                more = lax.dot_general(
                    jnp.concatenate(highs, axis=0), band_l[r], NT,
                    preferred_element_type=jnp.float32,
                )
                tall = 2 * levels
                total = main[: blocks * tall] + main[blocks * tall :] + more
                for b in range(blocks):
                    width = min(BLOCK, cols - b * BLOCK)
                    part = total[b * tall : (b + 1) * tall, :width]
                    store_winds(step, r, part[:levels], part[levels:], b * BLOCK, width)
                return carry

            lax.fori_loop(0, rows, smooth, 0)

        @pl.when(inner)
        def _():
            after, before = upright(cols_e[phase]), upright(cols_w[phase])

            def plain(r, carry):
                change = lon_difference(p_tall[step, r + 1], take(before, r), take(after, r))
                tend_u = -metric_ref[r] * change
                tend_v = (-meridional * 0.5) * (p_tall[step, r + 2] - p_tall[step, r])
                store_winds(step, r, tend_u[:, :cols], tend_v[:, :cols], 0, cols)
                return carry

            lax.fori_loop(0, rows, plain, 0)

        phase = phase + 1
        tall_rows(phase, v_tall.at[step], "start")
        if step == 0:
            tile_of = lambda r, base: u_wide[r, :, base : base + 128]
        else:
            def copy_u(r, carry):
                u_wide[r, :, 0:cols] = u_out[r]
                return carry

            lax.fori_loop(0, rows, copy_u, 0)
            tile_of = lambda r, base: u_wide[r, :, base : base + 128]
        send_cols[phase, 0] = column_of(tile_of, 0)
        send_cols[phase, 1] = column_of(tile_of, cols - 1)
        columns(phase, "start")
        columns(phase, "recv")
        tall_rows(phase, v_tall.at[step], "recv")

        @pl.when(first)
        def _():
            v_tall[step, 0] = -v_tall[step, 0]

        @pl.when(final)
        def _():
            v_tall[step, rows + 1] = -v_tall[step, rows + 1]

        after, before = upright(cols_e[phase]), upright(cols_w[phase])

        def solve(r, carry):
            change = lon_difference(u_wide[r], take(before, r), take(after, r))
            divergence = metric_ref[r] * change + (meridional * 0.5) * (
                v_tall[step, r + 2] - v_tall[step, r]
            )
            source = p_tall[step, r + 1] - compress * divergence
            source = jnp.concatenate(
                [source, jnp.zeros((8, padded), jnp.float32)], axis=0
            )
            high, low = split(source)
            stacked = jnp.concatenate([high, low, high], axis=0)
            result = lax.dot_general(
                helm_ref[r].astype(jnp.bfloat16), stacked, (((1,), (0,)), ((), ())),
                preferred_element_type=jnp.float32,
            )
            if step == 0:
                p_tall[1, r + 1] = result
            else:
                p_out[r] = result[:, :cols]
                v_out[r] = v_tall[1, r + 1, :, 0:cols]
            return carry

        lax.fori_loop(0, rows, solve, 0)

    for step in range(2):
        tall_rows(2 * step, p_tall.at[step], "send")
        wide_sides(step, "send")
        columns(2 * step, "send")
        tall_rows(2 * step + 1, v_tall.at[step], "send")
        columns(2 * step + 1, "send")


def on_device(zonal, merid, pressure, zonal_metric, helm_inverse, kernel_taps, filter_width):
    rows, levels, cols = pressure.shape
    half = kernel_taps.shape[1] // 2
    padded = -(-cols // 128) * 128
    lats, lons = lax.axis_size("lat"), lax.axis_size("lon")
    weights = kernels(kernel_taps, filter_width)
    weights = jnp.where(lax.axis_index("lat") == 0, weights[:rows], weights[rows:])
    weights = jnp.pad(weights, ((0, 0), (0, BLOCK)))
    high = lax.reduce_precision(helm_inverse, 8, 7)
    gap = jnp.zeros((rows, levels, 8), jnp.float32)
    helm = jnp.concatenate([high, gap, high, gap, helm_inverse - high, gap], axis=2)
    sizes = (rows, levels, cols, half, lats, lons)
    vmem = pl.BlockSpec(memory_space=pltpu.VMEM)
    field = jax.ShapeDtypeStruct((rows, levels, cols), jnp.float32)
    return pl.pallas_call(
        functools.partial(kernel, sizes),
        out_shape=(field, field, field),
        in_specs=[vmem, vmem, vmem, pl.BlockSpec(memory_space=pltpu.SMEM), vmem, vmem],
        out_specs=(vmem, vmem, vmem),
        scratch_shapes=[
            pltpu.VMEM((2, rows + 2, levels, padded), jnp.float32),
            pltpu.VMEM((2, rows + 2, levels, padded), jnp.float32),
            pltpu.VMEM((rows, levels, padded), jnp.float32),
            pltpu.VMEM((2, rows + 2, levels, half), jnp.float32),
            pltpu.VMEM((2, rows + 2, levels, half), jnp.float32),
            pltpu.VMEM((2, rows, levels, half), jnp.float32),
            pltpu.VMEM((4, rows, levels), jnp.float32),
            pltpu.VMEM((4, rows, levels), jnp.float32),
            pltpu.VMEM((4, 2, rows, levels), jnp.float32),
            pltpu.VMEM((rows, BLOCK, 2 * half + BLOCK), jnp.bfloat16),
            pltpu.VMEM((rows, BLOCK, 2 * half + BLOCK), jnp.bfloat16),
            pltpu.SemaphoreType.DMA((4, 11)),
            pltpu.SemaphoreType.DMA((4, 11)),
        ],
        compiler_params=pltpu.CompilerParams(
            collective_id=0, has_side_effects=True, vmem_limit_bytes=58 * 1024 * 1024
        ),
    )(zonal, merid, pressure, zonal_metric, helm, weights)


def solution(mesh):
    field = P("lat", None, "lon")
    return jax.shard_map(
        on_device,
        mesh=mesh,
        in_specs=(field, field, field, P("lat"), P("lat", None, None), P(), P()),
        out_specs=(field, field, field),
        check_vma=False,
    )
```

time: 198 us -> 105 us (0.53)
  Pallas kernels: 0 us -> 93.3 us
  waiting for transfers between devices: 65.7 us -> 0 us
  local copies, waits for them, and re-layouts: 42.6 us -> 8.27 us
  starting transfers between devices: 33.5 us -> 0 us
  matrix products: 26.1 us -> 0 us
  other arithmetic: 28.5 us -> 2.8 us
    pallas_call x0 -> x1, Pallas kernels: none -> 93.3 us  [on_device(): pl.pallas_call(functools.partial(kernel, sizes), out_shape=(field, field,...]
    ppermute x20 -> x0, waiting for transfers between devices: 65.7 us -> none  [the longest x4 31.2 us: lon_sides(): after = lax.ppermute(values[..., :width], 'lon', [(j, i) for i, j in up])]
    ppermute x20 -> x0, starting transfers between devices: 33.5 us -> none  [the longest x4 14.2 us: pole_rows(): partner = sign_flip * lax.ppermute(edge, ('lat', 'lon'), route)]
    dot_general x4 -> x0, matrix products: 26.1 us -> none  [the longest x2 21.2 us: on_device(): jnp.einsum('rbvk,rok->rvbo', windows, band, precision=lax.Precision.HIGH)]
    another operation x4 -> x0, local copies, waits for them, and re-layouts: 16.9 us -> none  [the longest x2 12.7 us: toeplitz(): tiled = jnp.tile(padded, (1, outputs))[:, :outputs * (outputs + taps)]]
    mul x3 -> x0, other arithmetic: 14.1 us -> none  [the longest x2 14.1 us: on_device(): tend_v = -meridional * 0.5 * (wide[2:, :, 1:-1] - wide[:-2, :, 1:-1])]
    concatenate x3 -> x1, local copies, waits for them, and re-layouts: 9.15 us -> 1.39 us  [on_device(): jnp.concatenate([high, gap, high, gap, helm_inverse - high, gap], axis=2)]
    another operation x2 -> x0, other arithmetic: 7.54 us -> none  [on_device(): jnp.stack([padded[..., b * BLOCK:b * BLOCK + BLOCK + taps] for b in range...]
  transfers between devices with their start and end apart: 20 -> 0, of which waited for: 17 -> 0; matrix products, arithmetic and copies ran while one was open for 10% -> 0% of each run, Pallas kernels for 0% -> 0%
where the time goes in v2:
time: 105 us
  Pallas kernels  93.3 us (89%)
  local copies, waits for them, and re-layouts  8.27 us (8%)
  other arithmetic  2.8 us (3%)
    pallas_call x1, Pallas kernels, on_device(): pl.pallas_call(functools.partial(kernel, sizes), out_shape=(field, field,...  93.3 us
    unnamed x7, local copies, waits for them, and re-layouts  6.25 us

profile of v2, /device:TPU:0, one launch (start us, length us, event | category | flops | bytes accessed | tf_op | source)
XLA Modules:
  0.0 105.0 jit_solution(12522248148386793253)
XLA Ops:
  0.6 0.9 fusion.1
  1.6 0.8 fusion
  2.4 0.6 pad.4.weight_ref
  3.1 1.0 reduce-precision_subtract_fusion
  4.1 1.4 %concatenate.3.helm_ref = f32[8,72,240]{2,1,0:T(8,128)} concatenate(f32[8,72,72]{2,1,0:T(8,128)S(1)} %get-tuple-element.4, f32[8,72,8]{2,1,0:T(8,128)S(1)} %broadcast_in_dim.4, f32[8,72,72]{2,1,0:T(8,128)S(1)} %get-tuple-element.4, f32[8,72,8]{2,1,0:T(8,128)S(1)} %broadcast_in_dim.4, f32[8,72,72]{2,1,0:T(8,128)S(1)} %get-tuple-element.3, f32[8,72,8]{2,1,0:T(8,128)S(1)} %broadcast_in_dim.4), dimensions={2} | concatenate | bytes 1105920 | tf_op jit(solution)/shard_map/concatenate | solution.py:421
  5.5 93.3 %shard_map.94 = (f32[8,72,720]{2,1,0:T(8,128)}, f32[8,72,720]{2,1,0:T(8,128)}, f32[8,72,720]{2,1,0:T(8,128)}) custom-call(f32[8,72,720]{2,1,0:T(8,128)} %u_in.1, f32[8,72,720]{2,1,0:T(8,128)} %v_in.1, f32[8,72,720]{2,1,0:T(8,128)} %p_in.1, f32[8]{0:T(128)} %metric_ref.1, f32[8,72,240]{2,1,0:T(8,128)} %concatenate.3.helm_ref, f32[8,768]{1,0:T(8,128)} %pad.4.weight_ref), custom_call_target="tpu_custom_call" | custom-call | tf_op jit(solution)/shard_map/pallas_call | solution.py:425
  98.8 0.0 copy-start.1
  98.8 2.9 %copy.13 = f32[8,72,720]{2,1,0:T(8,128)} copy(f32[8,72,720]{2,1,0:T(8,128)} %get-tuple-element.8) | data formatting | bytes 3317760
  101.7 0.0 copy-done.1
  101.7 0.0 copy-start
  101.7 1.2 %copy.14 = f32[8,72,720]{2,1,0:T(8,128)} copy(f32[8,72,720]{2,1,0:T(8,128)S(1)} %copy-done.1) | data formatting | bytes 3317760
  102.9 0.9 copy-done
  103.8 1.2 %copy.15 = f32[8,72,720]{2,1,0:T(8,128)} copy(f32[8,72,720]{2,1,0:T(8,128)S(1)} %copy-done) | data formatting | bytes 3317760
  (3 shorter events, 0.0 us)
Async XLA Ops:
  98.8 2.9 %copy-start.1 = (f32[8,72,720]{2,1,0:T(8,128)S(1)}, f32[8,72,720]{2,1,0:T(8,128)}, u32[]{:S(2)}) copy-start(f32[8,72,720]{2,1,0:T(8,128)} %get-tuple-element.9) | copy-start | bytes 4976644
  101.7 2.1 %copy-start = (f32[8,72,720]{2,1,0:T(8,128)S(1)}, f32[8,72,720]{2,1,0:T(8,128)}, u32[]{:S(2)}) copy-start(f32[8,72,720]{2,1,0:T(8,128)} %get-tuple-element.10) | copy-start | bytes 4976644

commit v3 on v2

--- a/solution.py
+++ b/solution.py
@@ -14,15 +14,7 @@
 NT = (((1,), (1,)), ((), ()))
 EXACT = lax.Precision.HIGHEST
 SOUTH, NORTH, COL_E, COL_W, WIDE_W, WIDE_E, RIM_W0, RIM_E0, RIM_W9, RIM_E9 = range(10)
-
-
-def kernels(kernel_taps, filter_width):
-    tap_count = kernel_taps.shape[1]
-    offsets = jnp.abs(jnp.arange(tap_count, dtype=jnp.int32) - tap_count // 2)
-    kept_taps = jnp.where(
-        offsets[None, :] <= filter_width[:, None], kernel_taps, jnp.zeros_like(kernel_taps)
-    )
-    return kept_taps / jnp.sum(kept_taps, axis=1, keepdims=True)
+OVER, MID_W, MID_E, TOP_W, TOP_E = range(10, 15)
 
 
 def split(value):
@@ -31,7 +23,7 @@
 
 
 def kernel(
-    sizes, u_in, v_in, p_in, metric_ref, helm_ref, weight_ref, u_out, v_out, p_out,
+    sizes, u_in, v_in, p_in, metric_ref, helm_ref, taps_ref, width_ref, u_out, v_out, p_out,
     p_tall, v_tall, u_wide, west, east, stage, cols_e, cols_w, send_cols, band_h, band_l,
     send_sem, recv_sem,
 ):
@@ -106,8 +98,8 @@
     def tall_rows(phase, tall, act):
         up = copy(phase, SOUTH, tall.at[rows], tall.at[0], (lat + 1, lon))
         down = copy(phase, NORTH, tall.at[1], tall.at[rows + 1], (lat - 1, lon))
-        over0 = copy(phase, RIM_W0 + 4, tall.at[1], tall.at[0], (lat, shift(across)))
-        over9 = copy(phase, RIM_W0 + 4, tall.at[rows], tall.at[rows + 1], (lat, shift(across)))
+        over0 = copy(phase, OVER, tall.at[1], tall.at[0], (lat, shift(across)))
+        over9 = copy(phase, OVER, tall.at[rows], tall.at[rows + 1], (lat, shift(across)))
         if act == "start":
             pl.when(first)(over0.start)
             pl.when(final)(over9.start)
@@ -135,25 +127,10 @@
             else:
                 one.wait_send()
 
-    def wide_sides(step, act):
+    def wide_sides(step, act, part=None):
         phase = 2 * step
         tall = p_tall.at[step]
         side = stage.at[step]
-
-        @pl.when(polar)
-        def _():
-            up = copy(phase, WIDE_W, side, west.at[step, pl.ds(1, rows)], (lat, shift(1)))
-            down = copy(
-                phase, WIDE_E, tall.at[pl.ds(1, rows), :, pl.ds(0, half)],
-                east.at[step, pl.ds(1, rows)], (lat, shift(-1)),
-            )
-            for one in (up, down):
-                if act == "start":
-                    one.start()
-                elif act == "recv":
-                    one.wait_recv()
-                else:
-                    one.wait_send()
 
         def rims(row, slot, kind, lat_to, lon_w, lon_e):
             to_west = copy(
@@ -178,16 +155,41 @@
         own9 = rims(rows - 1, rows + 1, RIM_W9, lat, shift(1 - across), shift(-1 - across))
         to_first = rims(0, rows + 1, RIM_W9, 0, shift(1), shift(-1))
         to_final = rims(rows - 1, 0, RIM_W0, lats - 1, shift(1), shift(-1))
+
+        def chunk(start, count, kind):
+            up = copy(
+                phase, kind, side.at[pl.ds(start, count)],
+                west.at[step, pl.ds(start + 1, count)], (lat, shift(1)),
+            )
+            down = copy(
+                phase, kind + 1, tall.at[pl.ds(start + 1, count), :, pl.ds(0, half)],
+                east.at[step, pl.ds(start + 1, count)], (lat, shift(-1)),
+            )
+            return up, down
+
+        low = chunk(0, 2, WIDE_W)
+        high = chunk(rows - 2, 2, TOP_W)
+        middle = chunk(2, rows - 4, MID_W)
         if act == "recv":
+            if part == "edge":
+                run(own0)
+                run(own9)
+                run(low)
+                run(high)
+            else:
+                run(middle)
+        elif part == "middle":
+            pl.when(polar)(lambda: run(middle))
+        else:
+            pl.when(lat == 1)(lambda: run(to_first))
+            pl.when(lat == lats - 2)(lambda: run(to_final))
+            pl.when(first)(lambda: run(own0))
+            pl.when(final)(lambda: run(own9))
+
             @pl.when(polar)
             def _():
-                run(own0)
-                run(own9)
-        else:
-            pl.when(first)(lambda: run(own0))
-            pl.when(final)(lambda: run(own9))
-            pl.when(lat == 1)(lambda: run(to_first))
-            pl.when(lat == lats - 2)(lambda: run(to_final))
+                run(low)
+                run(high)
 
     lane = lax.broadcasted_iota(jnp.int32, (rows, 128), 1)
     sub = lax.broadcasted_iota(jnp.int32, (rows, 128), 0)
@@ -261,7 +263,7 @@
 
             lax.fori_loop(0, rows, edge, 0)
 
-        wide_sides(step, "start")
+        wide_sides(step, "start", "edge")
         tile_of = lambda r, base: p_tall[step, r + 1, :, base : base + 128]
         send_cols[phase, 0] = column_of(tile_of, 0)
 
@@ -274,14 +276,15 @@
             send_cols[phase, 1] = column_of(tile_of, cols - 1)
 
         columns(phase, "start")
+        wide_sides(step, "start", "middle")
 
     def store_winds(step, r, add_u, add_v, base, width):
         at = slice(base, base + width)
         if step == 0:
-            u_wide[r, :, at] = u_in[r, :, at] + add_u
+            u_wide[0, r, :, at] = u_in[r, :, at] + add_u
             v_tall[0, r + 1, :, at] = v_in[r, :, at] + add_v
         else:
-            u_out[r, :, at] = u_wide[r, :, at] + add_u
+            u_wide[1, r, :, at] = u_wide[0, r, :, at] + add_u
             v_tall[1, r + 1, :, at] = v_tall[0, r + 1, :, at] + add_v
 
     for step in range(2):
@@ -291,21 +294,24 @@
             @pl.when(polar)
             def _():
                 def build(r, carry):
-                    line = jnp.broadcast_to(
-                        weight_ref[pl.ds(r, 1), :], (BLOCK, 2 * half + BLOCK)
-                    )
+                    q = r + jnp.where(first, 0, rows)
+                    away = jnp.abs(lax.broadcasted_iota(jnp.int32, (1, 2 * half), 1) - half)
+                    kept = jnp.where(away <= width_ref[q], taps_ref[pl.ds(q, 1), :], 0.0)
+                    kept = kept / jnp.sum(kept, axis=1, keepdims=True)
+                    line = jnp.concatenate([kept, jnp.zeros((1, BLOCK), jnp.float32)], axis=1)
+                    line = jnp.broadcast_to(line, (BLOCK, 2 * half + BLOCK))
                     matrix = pltpu.roll(line, 0, 1, stride=1, stride_axis=0)
                     band_h[r], band_l[r] = split(matrix)
                     return carry
 
                 lax.fori_loop(0, rows, build, 0)
 
+        columns(phase, "recv")
         tall_rows(phase, p_tall.at[step], "recv")
-        columns(phase, "recv")
 
         @pl.when(polar)
         def _():
-            wide_sides(step, "recv")
+            wide_sides(step, "recv", "edge")
             far = upright(cols_w[phase])
 
             def smooth(r, carry):
@@ -334,7 +340,10 @@
                     store_winds(step, r, part[:levels], part[levels:], b * BLOCK, width)
                 return carry
 
-            lax.fori_loop(0, rows, smooth, 0)
+            lax.fori_loop(0, 2, lambda i, c: smooth(i * (rows - 1), c), 0)
+            tall_rows(phase + 1, v_tall.at[step], "start")
+            wide_sides(step, "recv", "middle")
+            lax.fori_loop(1, rows - 1, smooth, 0)
 
         @pl.when(inner)
         def _():
@@ -347,62 +356,59 @@
                 store_winds(step, r, tend_u[:, :cols], tend_v[:, :cols], 0, cols)
                 return carry
 
-            lax.fori_loop(0, rows, plain, 0)
+            lax.fori_loop(0, 2, lambda i, c: plain(i * (rows - 1), c), 0)
+            tall_rows(phase + 1, v_tall.at[step], "start")
+            lax.fori_loop(1, rows - 1, plain, 0)
 
         phase = phase + 1
-        tall_rows(phase, v_tall.at[step], "start")
-        if step == 0:
-            tile_of = lambda r, base: u_wide[r, :, base : base + 128]
-        else:
-            def copy_u(r, carry):
-                u_wide[r, :, 0:cols] = u_out[r]
-                return carry
-
-            lax.fori_loop(0, rows, copy_u, 0)
-            tile_of = lambda r, base: u_wide[r, :, base : base + 128]
+        tile_of = lambda r, base: u_wide[step, r, :, base : base + 128]
         send_cols[phase, 0] = column_of(tile_of, 0)
         send_cols[phase, 1] = column_of(tile_of, cols - 1)
         columns(phase, "start")
         columns(phase, "recv")
-        tall_rows(phase, v_tall.at[step], "recv")
-
-        @pl.when(first)
-        def _():
-            v_tall[step, 0] = -v_tall[step, 0]
-
-        @pl.when(final)
-        def _():
-            v_tall[step, rows + 1] = -v_tall[step, rows + 1]
-
         after, before = upright(cols_e[phase]), upright(cols_w[phase])
 
         def solve(r, carry):
-            change = lon_difference(u_wide[r], take(before, r), take(after, r))
+            change = lon_difference(u_wide[step, r], take(before, r), take(after, r))
             divergence = metric_ref[r] * change + (meridional * 0.5) * (
                 v_tall[step, r + 2] - v_tall[step, r]
             )
             source = p_tall[step, r + 1] - compress * divergence
-            source = jnp.concatenate(
-                [source, jnp.zeros((8, padded), jnp.float32)], axis=0
-            )
             high, low = split(source)
-            stacked = jnp.concatenate([high, low, high], axis=0)
-            result = lax.dot_general(
-                helm_ref[r].astype(jnp.bfloat16), stacked, (((1,), (0,)), ((), ())),
-                preferred_element_type=jnp.float32,
-            )
+            inverse = helm_ref[r]
+            inverse_high = inverse.astype(jnp.bfloat16).astype(jnp.float32)
+            both = jnp.concatenate([inverse_high, inverse - inverse_high], axis=0)
+            product = lax.dot_general(
+                both.astype(jnp.bfloat16), jnp.concatenate([high, low], axis=1),
+                (((1,), (0,)), ((), ())), preferred_element_type=jnp.float32,
+            )
+            result = product[:levels, :padded] + product[:levels, padded:]
+            result = result + product[levels:, :padded]
             if step == 0:
                 p_tall[1, r + 1] = result
             else:
                 p_out[r] = result[:, :cols]
                 v_out[r] = v_tall[1, r + 1, :, 0:cols]
+                u_out[r] = u_wide[1, r, :, 0:cols]
             return carry
 
-        lax.fori_loop(0, rows, solve, 0)
+        lax.fori_loop(1, rows - 1, solve, 0)
+        tall_rows(phase, v_tall.at[step], "recv")
+
+        @pl.when(first)
+        def _():
+            v_tall[step, 0] = -v_tall[step, 0]
+
+        @pl.when(final)
+        def _():
+            v_tall[step, rows + 1] = -v_tall[step, rows + 1]
+
+        lax.fori_loop(0, 2, lambda i, c: solve(i * (rows - 1), c), 0)
 
     for step in range(2):
         tall_rows(2 * step, p_tall.at[step], "send")
-        wide_sides(step, "send")
+        wide_sides(step, "send", "edge")
+        wide_sides(step, "send", "middle")
         columns(2 * step, "send")
         tall_rows(2 * step + 1, v_tall.at[step], "send")
         columns(2 * step + 1, "send")
@@ -413,24 +419,19 @@
     half = kernel_taps.shape[1] // 2
     padded = -(-cols // 128) * 128
     lats, lons = lax.axis_size("lat"), lax.axis_size("lon")
-    weights = kernels(kernel_taps, filter_width)
-    weights = jnp.where(lax.axis_index("lat") == 0, weights[:rows], weights[rows:])
-    weights = jnp.pad(weights, ((0, 0), (0, BLOCK)))
-    high = lax.reduce_precision(helm_inverse, 8, 7)
-    gap = jnp.zeros((rows, levels, 8), jnp.float32)
-    helm = jnp.concatenate([high, gap, high, gap, helm_inverse - high, gap], axis=2)
     sizes = (rows, levels, cols, half, lats, lons)
+    smem = pl.BlockSpec(memory_space=pltpu.SMEM)
     vmem = pl.BlockSpec(memory_space=pltpu.VMEM)
     field = jax.ShapeDtypeStruct((rows, levels, cols), jnp.float32)
     return pl.pallas_call(
         functools.partial(kernel, sizes),
         out_shape=(field, field, field),
-        in_specs=[vmem, vmem, vmem, pl.BlockSpec(memory_space=pltpu.SMEM), vmem, vmem],
+        in_specs=[vmem, vmem, vmem, smem, vmem, vmem, smem],
         out_specs=(vmem, vmem, vmem),
         scratch_shapes=[
             pltpu.VMEM((2, rows + 2, levels, padded), jnp.float32),
             pltpu.VMEM((2, rows + 2, levels, padded), jnp.float32),
-            pltpu.VMEM((rows, levels, padded), jnp.float32),
+            pltpu.VMEM((2, rows, levels, padded), jnp.float32),
             pltpu.VMEM((2, rows + 2, levels, half), jnp.float32),
             pltpu.VMEM((2, rows + 2, levels, half), jnp.float32),
             pltpu.VMEM((2, rows, levels, half), jnp.float32),
@@ -439,13 +440,13 @@
             pltpu.VMEM((4, 2, rows, levels), jnp.float32),
             pltpu.VMEM((rows, BLOCK, 2 * half + BLOCK), jnp.bfloat16),
             pltpu.VMEM((rows, BLOCK, 2 * half + BLOCK), jnp.bfloat16),
-            pltpu.SemaphoreType.DMA((4, 11)),
-            pltpu.SemaphoreType.DMA((4, 11)),
+            pltpu.SemaphoreType.DMA((4, 15)),
+            pltpu.SemaphoreType.DMA((4, 15)),
         ],
         compiler_params=pltpu.CompilerParams(
             collective_id=0, has_side_effects=True, vmem_limit_bytes=58 * 1024 * 1024
         ),
-    )(zonal, merid, pressure, zonal_metric, helm, weights)
+    )(zonal, merid, pressure, zonal_metric, helm_inverse, kernel_taps, filter_width)
 
 
 def solution(mesh):

time: 105 us -> 89.1 us (0.85)
  Pallas kernels: 93.3 us -> 82.1 us
  other arithmetic: 2.8 us -> 0 us
  local copies, waits for them, and re-layouts: 8.27 us -> 6.25 us
    pallas_call x1, Pallas kernels: 93.3 us -> 82.1 us  [on_device(): pl.pallas_call(functools.partial(kernel, sizes), out_shape=(field, field,...]
    concatenate x1 -> x0, local copies, waits for them, and re-layouts: 1.39 us -> none  [on_device(): jnp.concatenate([high, gap, high, gap, helm_inverse - high, gap], axis=2)]
where the time goes in v3:
time: 89.1 us; the launch traced here: 89 us
  Pallas kernels  82.1 us (92%)
  local copies, waits for them, and re-layouts  6.25 us (7%)
    pallas_call x1, Pallas kernels, on_device(): pl.pallas_call(functools.partial(kernel, sizes), out_shape=(field, field,...  82.1 us
    unnamed x7, local copies, waits for them, and re-layouts  6.25 us

profile of v3, /device:TPU:0, one launch (start us, length us, event | category | flops | bytes accessed | tf_op | source)
XLA Modules:
  0.0 89.0 jit_solution(2432896462856529143)
XLA Ops:
  0.6 82.1 %shard_map.94 = (f32[8,72,720]{2,1,0:T(8,128)}, f32[8,72,720]{2,1,0:T(8,128)}, f32[8,72,720]{2,1,0:T(8,128)}) custom-call(f32[8,72,720]{2,1,0:T(8,128)} %u_in.1, f32[8,72,720]{2,1,0:T(8,128)} %v_in.1, f32[8,72,720]{2,1,0:T(8,128)} %p_in.1, f32[8]{0:T(128)} %metric_ref.1, f32[8,72,72]{2,1,0:T(8,128)} %helm_ref.1, f32[16,512]{1,0:T(8,128)} %taps_ref.1, ...), custom_call_target="tpu_custom_call" | custom-call | tf_op jit(solution)/shard_map/pallas_call | solution.py:426
  82.7 0.0 copy-start.1
  82.7 2.9 %copy.13 = f32[8,72,720]{2,1,0:T(8,128)} copy(f32[8,72,720]{2,1,0:T(8,128)} %get-tuple-element.6) | data formatting | bytes 3317760
  85.6 0.0 copy-done.1
  85.6 0.0 copy-start
  85.6 1.2 %copy.14 = f32[8,72,720]{2,1,0:T(8,128)} copy(f32[8,72,720]{2,1,0:T(8,128)S(1)} %copy-done.1) | data formatting | bytes 3317760
  86.8 0.9 %copy-done = f32[8,72,720]{2,1,0:T(8,128)S(1)} copy-done((f32[8,72,720]{2,1,0:T(8,128)S(1)}, f32[8,72,720]{2,1,0:T(8,128)}, u32[]{:S(2)}) %copy-start) | copy-done | bytes 1658904
  87.7 1.2 %copy.15 = f32[8,72,720]{2,1,0:T(8,128)} copy(f32[8,72,720]{2,1,0:T(8,128)S(1)} %copy-done) | data formatting | bytes 3317760
Async XLA Ops:
  82.7 2.9 %copy-start.1 = (f32[8,72,720]{2,1,0:T(8,128)S(1)}, f32[8,72,720]{2,1,0:T(8,128)}, u32[]{:S(2)}) copy-start(f32[8,72,720]{2,1,0:T(8,128)} %get-tuple-element.7) | copy-start | bytes 4976644
  85.6 2.1 %copy-start = (f32[8,72,720]{2,1,0:T(8,128)S(1)}, f32[8,72,720]{2,1,0:T(8,128)}, u32[]{:S(2)}) copy-start(f32[8,72,720]{2,1,0:T(8,128)} %get-tuple-element.8) | copy-start | bytes 4976644

commit v4 on v3

--- a/solution.py
+++ b/solution.py
@@ -14,7 +14,7 @@
 NT = (((1,), (1,)), ((), ()))
 EXACT = lax.Precision.HIGHEST
 SOUTH, NORTH, COL_E, COL_W, WIDE_W, WIDE_E, RIM_W0, RIM_E0, RIM_W9, RIM_E9 = range(10)
-OVER, MID_W, MID_E, TOP_W, TOP_E = range(10, 15)
+OVER, TOP_W, TOP_E, MIDDLE = range(10, 14)
 
 
 def split(value):
@@ -169,17 +169,27 @@
 
         low = chunk(0, 2, WIDE_W)
         high = chunk(rows - 2, 2, TOP_W)
-        middle = chunk(2, rows - 4, MID_W)
+
+        def middle(i, carry):
+            run(chunk(2 + i, 1, MIDDLE + 2 * i))
+            return carry
+
         if act == "recv":
-            if part == "edge":
+            if isinstance(part, str):
                 run(own0)
                 run(own9)
                 run(low)
                 run(high)
             else:
-                run(middle)
-        elif part == "middle":
-            pl.when(polar)(lambda: run(middle))
+                middle(part, 0)
+        elif isinstance(part, str) and part == "middle":
+
+
+            @pl.when(polar)
+            def _():
+                lax.fori_loop(0, rows - 4, middle, 0)
+
+
         else:
             pl.when(lat == 1)(lambda: run(to_first))
             pl.when(lat == lats - 2)(lambda: run(to_final))
@@ -342,8 +352,13 @@
 
             lax.fori_loop(0, 2, lambda i, c: smooth(i * (rows - 1), c), 0)
             tall_rows(phase + 1, v_tall.at[step], "start")
-            wide_sides(step, "recv", "middle")
-            lax.fori_loop(1, rows - 1, smooth, 0)
+
+            def arrive(i, carry):
+                wide_sides(step, "recv", i)
+                return smooth(i + 1, carry)
+
+            lax.fori_loop(0, rows - 4, arrive, 0)
+            lax.fori_loop(rows - 3, rows - 1, smooth, 0)
 
         @pl.when(inner)
         def _():
@@ -440,8 +455,8 @@
             pltpu.VMEM((4, 2, rows, levels), jnp.float32),
             pltpu.VMEM((rows, BLOCK, 2 * half + BLOCK), jnp.bfloat16),
             pltpu.VMEM((rows, BLOCK, 2 * half + BLOCK), jnp.bfloat16),
-            pltpu.SemaphoreType.DMA((4, 15)),
-            pltpu.SemaphoreType.DMA((4, 15)),
+            pltpu.SemaphoreType.DMA((4, 5 + 2 * rows)),
+            pltpu.SemaphoreType.DMA((4, 5 + 2 * rows)),
         ],
         compiler_params=pltpu.CompilerParams(
             collective_id=0, has_side_effects=True, vmem_limit_bytes=58 * 1024 * 1024

time: 89.1 us -> 83.7 us (0.939)
  Pallas kernels: 82.1 us -> 76.6 us
    pallas_call x1, Pallas kernels: 82.1 us -> 76.6 us  [on_device(): pl.pallas_call(functools.partial(kernel, sizes), out_shape=(field, field,...]
where the time goes in v4:
time: 83.7 us; the launch traced here: 83.5 us
  Pallas kernels  76.6 us (92%)
  local copies, waits for them, and re-layouts  6.25 us (7%)
    pallas_call x1, Pallas kernels, on_device(): pl.pallas_call(functools.partial(kernel, sizes), out_shape=(field, field,...  76.6 us
    unnamed x7, local copies, waits for them, and re-layouts  6.25 us

profile of v4, /device:TPU:0, one launch (start us, length us, event | category | flops | bytes accessed | tf_op | source)
XLA Modules:
  0.0 83.5 jit_solution(1718221530273433853)
XLA Ops:
  0.6 76.6 %shard_map.94 = (f32[8,72,720]{2,1,0:T(8,128)}, f32[8,72,720]{2,1,0:T(8,128)}, f32[8,72,720]{2,1,0:T(8,128)}) custom-call(f32[8,72,720]{2,1,0:T(8,128)} %u_in.1, f32[8,72,720]{2,1,0:T(8,128)} %v_in.1, f32[8,72,720]{2,1,0:T(8,128)} %p_in.1, f32[8]{0:T(128)} %metric_ref.1, f32[8,72,72]{2,1,0:T(8,128)} %helm_ref.1, f32[16,512]{1,0:T(8,128)} %taps_ref.1, ...), custom_call_target="tpu_custom_call" | custom-call | tf_op jit(solution)/shard_map/pallas_call | solution.py:441
  77.3 0.0 copy-start.1
  77.3 2.9 %copy.13 = f32[8,72,720]{2,1,0:T(8,128)} copy(f32[8,72,720]{2,1,0:T(8,128)} %get-tuple-element.6) | data formatting | bytes 3317760
  80.2 0.0 copy-done.1
  80.2 0.0 copy-start
  80.2 1.2 %copy.14 = f32[8,72,720]{2,1,0:T(8,128)} copy(f32[8,72,720]{2,1,0:T(8,128)S(1)} %copy-done.1) | data formatting | bytes 3317760
  81.4 0.9 %copy-done = f32[8,72,720]{2,1,0:T(8,128)S(1)} copy-done((f32[8,72,720]{2,1,0:T(8,128)S(1)}, f32[8,72,720]{2,1,0:T(8,128)}, u32[]{:S(2)}) %copy-start) | copy-done | bytes 1658904
  82.3 1.2 %copy.15 = f32[8,72,720]{2,1,0:T(8,128)} copy(f32[8,72,720]{2,1,0:T(8,128)S(1)} %copy-done) | data formatting | bytes 3317760
Async XLA Ops:
  77.3 2.9 %copy-start.1 = (f32[8,72,720]{2,1,0:T(8,128)S(1)}, f32[8,72,720]{2,1,0:T(8,128)}, u32[]{:S(2)}) copy-start(f32[8,72,720]{2,1,0:T(8,128)} %get-tuple-element.7) | copy-start | bytes 4976644
  80.2 2.1 %copy-start = (f32[8,72,720]{2,1,0:T(8,128)S(1)}, f32[8,72,720]{2,1,0:T(8,128)}, u32[]{:S(2)}) copy-start(f32[8,72,720]{2,1,0:T(8,128)} %get-tuple-element.8) | copy-start | bytes 4976644
